TPU v7x, 32 devices: a whole 2x2x4 slice. The times are simulated.
32 devices in a mesh: node: 16 (over z, y, x), board: 2 (over core).
Axes of the slice: x: 2, y: 2, z: 4, core: 2. Of those that a mesh axis runs over, the one named last changes fastest.
Arguments:
- logits: float32 [2, 4, 512, 1326], P('board', None, 'node'), may hold values from -310 to 310
- pot_size: float32 [4, 512], P(None, 'node'), may hold values from 1 to 20
- node_type: int32 [4, 512], P(None, 'node'), may hold values from 0 to 2, as said below
- parent_slot: int32 [4, 512], P(None, 'node'), may hold values from 0 to 511, as said below
- range_one: float32 [2, 1326], P('board'), may hold values from 0.05 to 1
- range_two: float32 [2, 1326], P('board'), may hold values from 0.05 to 1
- hand_rank: int32 [2, 1326], P('board'), may hold values from 0 to 7461
- live_mask: int32 [2, 1326], P('board'), may hold values 0 or 1
Outputs:
- new_logits: float32 [2, 4, 512, 1326], P('board', None, 'node')
- values_half: float32 [2, 4, 512, 1326], P('board', None, 'node')
Inputs may be any that keep to these rules, and one draw needn't show every extreme that they name: `node_type`: 0 marks an inner node. At each level but the last, each aligned group of four slots holds exactly one node of type 0; the last level holds none. `parent_slot`: at level 0 every entry is 0. At a level above 0 the four nodes of an aligned group of four share one parent, a node of type 0 at the level before, and every such node is the parent of exactly one group; the parent's group index is the group's own index minus an offset of 0 to 7, one offset a level, modulo 512 / 4.
All inputs are finite; a program needn't handle non-finite values. No bound on the sum of `live_mask` on one device may be relied on, other than what follows from the above.
Results may differ from a plain program's by a relative error of at most 0.0003.
Values sent between devices are 32-bit elements; how exact they have to be, the bound alone decides.
No kernel may reach another device: no remote copies, remote signals or barrier semaphores. Data moves between devices by JAX's collectives and lax.ppermute only.
A program may use at most 64 MiB of HBM per device.

v0:
```python
import jax
import jax.numpy as jnp
import numpy as np
from jax import lax
from jax.sharding import PartitionSpec as P

HANDS = 1326
LEVELS = 4
SLOT_DEV = 32


step_scale = 0.5
eps_value = 1e-06


def passed_along(value, axis, steps):
    count = lax.axis_size(axis)
    pairs = [(source, (source + steps) % count) for source in range(count)]
    return lax.ppermute(value, axis, pairs)


def card_pairs(hand_count):
    low_list = []
    high_list = []
    for low_card in range(52):
        for high_card in range(low_card + 1, 52):
            low_list.append(low_card)
            high_list.append(high_card)
    return (np.array(low_list[:hand_count], np.int32), np.array(high_list[:hand_count], np.int32))


def payoff_blocks(hand_rank, live_mask):
    low_np, high_np = card_pairs(hand_rank.shape[-1])
    low_card = jnp.asarray(low_np)
    high_card = jnp.asarray(high_np)
    clash_mask = (
        (low_card[:, None] == low_card[None, :])
        | (low_card[:, None] == high_card[None, :])
        | (high_card[:, None] == low_card[None, :])
        | (high_card[:, None] == high_card[None, :])
    )
    alive_flag = live_mask > 0
    keep_pair = jnp.logical_not(clash_mask)[None] & alive_flag[:, :, None] & alive_flag[:, None, :]
    higher = hand_rank[:, :, None] > hand_rank[:, None, :]
    lower = hand_rank[:, :, None] < hand_rank[:, None, :]
    order_value = jnp.where(higher, 1.0, jnp.where(lower, -1.0, 0.0))
    show_block = jnp.where(keep_pair, order_value, 0.0).astype(jnp.bfloat16)
    compat_block = jnp.where(keep_pair, 1.0, 0.0).astype(jnp.bfloat16)
    return (show_block, compat_block)


def policy(logits):
    full_shape = logits.shape
    grouped = logits.reshape(full_shape[0], full_shape[1], full_shape[2] // 4, 4, full_shape[3])
    return jax.nn.softmax(grouped, axis=3).reshape(full_shape)


def inner_position(kind_row):
    groups = SLOT_DEV // 4
    kind_grid = kind_row.reshape(groups, 4)
    return jnp.sum(jnp.where(kind_grid == 0, jnp.arange(4, dtype=jnp.int32)[None, :], 0), axis=1)


def reach_levels(strategy, parent_slot, node_type, range_one, range_two, start_slot):
    slot_count = SLOT_DEV * lax.axis_size("node")
    groups = SLOT_DEV // 4
    reach_one = range_one[:, None, :] * strategy[:, 0]
    reach_two = jnp.broadcast_to(range_two[:, None, :], reach_one.shape)
    list_one = [reach_one]
    list_two = [reach_two]
    for depth_idx in range(1, LEVELS):
        rel_slot = (parent_slot[depth_idx] - start_slot + SLOT_DEV) % slot_count
        inner_pos = inner_position(node_type[depth_idx - 1])
        tail_pos = 4 * jnp.arange(1, groups, dtype=jnp.int32) + inner_pos[1:]
        tail_one = jnp.take(reach_one, tail_pos, axis=1)
        tail_two = jnp.take(reach_two, tail_pos, axis=1)
        before_one, before_two = passed_along((tail_one, tail_two), "node", 1)
        local_idx = jnp.where(
            rel_slot >= SLOT_DEV, rel_slot - SLOT_DEV + groups - 1, rel_slot // 4 - 1
        )
        window_one = jnp.concatenate([before_one, reach_one], axis=1)
        window_two = jnp.concatenate([before_two, reach_two], axis=1)
        above_one = jnp.take(window_one, local_idx, axis=1)
        above_two = jnp.take(window_two, local_idx, axis=1)
        if depth_idx % 2 == 0:
            reach_one = above_one * strategy[:, depth_idx]
            reach_two = above_two
        else:
            reach_one = above_one
            reach_two = above_two * strategy[:, depth_idx]
        list_one.append(reach_one)
        list_two.append(reach_two)
    return (jnp.stack(list_one, axis=1), jnp.stack(list_two, axis=1))


def terminal_pay(reach_one, reach_two, pot_size, node_type, show_block, compat_block):
    boards = reach_one.shape[0]
    column_count = LEVELS * SLOT_DEV
    level_sign = jnp.where(jnp.arange(LEVELS) % 2 == 0, -1.0, 1.0).astype(jnp.float32)
    show_scale = jnp.where(node_type == 2, pot_size, 0.0)
    fold_scale = jnp.where(node_type == 1, pot_size, 0.0) * level_sign[:, None]

    def columns(reach_value, scale_value):
        return (
            (reach_value * scale_value[None, :, :, None])
            .astype(jnp.bfloat16)
            .reshape(boards, column_count, HANDS)
        )

    show_cols = jnp.concatenate(
        [columns(reach_two, show_scale), columns(reach_one, show_scale)], axis=1
    )
    fold_cols = jnp.concatenate(
        [columns(reach_two, fold_scale), -columns(reach_one, fold_scale)], axis=1
    )
    product = jnp.einsum(
        "bij,bnj->bni", show_block, show_cols, preferred_element_type=jnp.float32
    ) + jnp.einsum("bij,bnj->bni", compat_block, fold_cols, preferred_element_type=jnp.float32)
    pay_one = product[:, :column_count].reshape(boards, LEVELS, SLOT_DEV, HANDS)
    pay_two = product[:, column_count:].reshape(boards, LEVELS, SLOT_DEV, HANDS)
    return (pay_one, pay_two)


def values_up(strategy, parent_slot, node_type, pay_one, pay_two, start_slot):
    boards = strategy.shape[0]
    slot_count = SLOT_DEV * lax.axis_size("node")
    groups = SLOT_DEV // 4
    value_one = pay_one[:, LEVELS - 1]
    value_two = pay_two[:, LEVELS - 1]
    found_list = [None] * LEVELS
    found_list[LEVELS - 1] = value_two
    for depth_idx in range(LEVELS - 2, -1, -1):
        child_level = depth_idx + 1
        weight = strategy[:, child_level]
        if child_level % 2 == 0:
            term_one = weight * value_one
            term_two = value_two
        else:
            term_one = value_one
            term_two = weight * value_two
        group_one = term_one.reshape(boards, groups, 4, HANDS).sum(axis=2)
        group_two = term_two.reshape(boards, groups, 4, HANDS).sum(axis=2)
        parent_group = parent_slot[child_level].reshape(groups, 4)[:, 0]
        local_idx = (parent_group - start_slot + SLOT_DEV) % slot_count
        keeper = (jnp.arange(SLOT_DEV, 2 * SLOT_DEV)[:, None] == local_idx[None, :]).astype(
            jnp.float32
        )
        own_one = jnp.einsum("jg,bgh->bjh", keeper, group_one, precision=lax.Precision.HIGHEST)
        own_two = jnp.einsum("jg,bgh->bjh", keeper, group_two, precision=lax.Precision.HIGHEST)
        far_placer = (
            (local_idx[None, :] < SLOT_DEV)
            & (local_idx[None, :] // 4 - 1 == jnp.arange(groups - 1)[:, None])
        ).astype(jnp.float32)
        far_one = jnp.einsum("kg,bgh->bkh", far_placer, group_one, precision=lax.Precision.HIGHEST)
        far_two = jnp.einsum("kg,bgh->bkh", far_placer, group_two, precision=lax.Precision.HIGHEST)
        got_one, got_two = passed_along((far_one, far_two), "node", -1)
        kind_here = node_type[depth_idx]
        landing = (
            (jnp.arange(SLOT_DEV)[:, None] // 4 == jnp.arange(1, groups)[None, :])
            & (kind_here[:, None] == 0)
        ).astype(jnp.float32)
        sent_one = jnp.einsum("sk,bkh->bsh", landing, got_one, precision=lax.Precision.HIGHEST)
        sent_two = jnp.einsum("sk,bkh->bsh", landing, got_two, precision=lax.Precision.HIGHEST)
        value_one = pay_one[:, depth_idx] + (own_one + sent_one)
        value_two = pay_two[:, depth_idx] + (own_two + sent_two)
        found_list[depth_idx] = value_one if depth_idx % 2 == 0 else value_two
    return jnp.stack(found_list, axis=1)


def operate(
    point,
    pot_size,
    node_type,
    parent_slot,
    range_one,
    range_two,
    show_block,
    compat_block,
    start_slot,
):
    strategy = policy(point)
    reach_one, reach_two = reach_levels(
        strategy, parent_slot, node_type, range_one, range_two, start_slot
    )
    pay_one, pay_two = terminal_pay(
        reach_one, reach_two, pot_size, node_type, show_block, compat_block
    )
    return values_up(strategy, parent_slot, node_type, pay_one, pay_two, start_slot)


def rate_for(values_found):
    square_sum = lax.psum(jnp.sum(values_found * values_found), ("node", "board"))
    entry_count = values_found.size * lax.axis_size("node") * lax.axis_size("board")
    return step_scale / jnp.sqrt(square_sum / entry_count + eps_value)


def per_device(
    logits, pot_size, node_type, parent_slot, range_one, range_two, hand_rank, live_mask
):
    show_block, compat_block = payoff_blocks(hand_rank, live_mask)
    start_slot = lax.axis_index("node") * SLOT_DEV
    current = logits
    anchor_mix = 1.0 / 2
    base_point = current + anchor_mix * (logits - current)
    values_now = operate(
        current,
        pot_size,
        node_type,
        parent_slot,
        range_one,
        range_two,
        show_block,
        compat_block,
        start_slot,
    )
    half_point = base_point + rate_for(values_now) * values_now
    values_half = operate(
        half_point,
        pot_size,
        node_type,
        parent_slot,
        range_one,
        range_two,
        show_block,
        compat_block,
        start_slot,
    )
    current = base_point + rate_for(values_half) * values_half
    return (current, values_half)


def solution(mesh):
    return jax.shard_map(
        per_device,
        mesh=mesh,
        in_specs=(
            P("board", None, "node", None),
            P(None, "node"),
            P(None, "node"),
            P(None, "node"),
            P("board", None),
            P("board", None),
            P("board", None),
            P("board", None),
        ),
        out_specs=(P("board", None, "node", None), P("board", None, "node", None)),
        check_vma=False,
    )
```

profile of v0, /device:TPU:0, one launch (start us, length us, event | category | flops | bytes accessed | tf_op | source)
XLA Modules:
  0.0 261.7 jit_solution(468896531134147705)
XLA Ops:
  0.6 1.4 compare_bitcast_fusion.2
  2.3 0.7 reduce.16
  3.7 2.9 %collective-permute-start = (f32[1,7,1326]{2,1,0:T(8,128)S(1)}, f32[1,7,1326]{2,1,0:T(8,128)S(1)}, u32[]{:S(2)}, u32[]{:S(2)}) collective-permute-start(f32[1,7,1326]{2,1,0:T(8,128)S(1)} %bitcast_select_fusion.21), channel_id=1, source_target_pairs={{0,2},{2,4},{4,6},{6,8},{8,10},{10,12},{12,14},{14,16},{16,18},{18... | collective-permute-start | bytes 111392 | tf_op jit(solution)/shard_map/ppermute | solution.py:19
  6.7 1.3 reshape.1786
  14.5 0.6 gather_fusion.1
  15.9 1.5 collective-permute-start.1
  17.6 5.9 %collective-permute-done.1 = f32[1,7,1326]{2,1,0:T(8,128)S(1)} collective-permute-done((f32[1,7,1326]{2,1,0:T(8,128)S(1)}, f32[1,7,1326]{2,1,0:T(8,128)S(1)}, u32[]{:S(2)}, u32[]{:S(2)}) %collective-permute-start.1) | collective-permute-done | bytes 37160 | tf_op jit(solution)/shard_map/ppermute | solution.py:19
  25.0 7.5 %collective-permute-done.2 = f32[1,7,1326]{2,1,0:T(8,128)S(1)} collective-permute-done((f32[1,7,1326]{2,1,0:T(8,128)S(1)}, f32[1,7,1326]{2,1,0:T(8,128)S(1)}, u32[]{:S(2)}, u32[]{:S(2)}) %collective-permute-start.2) | collective-permute-done | bytes 37160 | tf_op jit(solution)/shard_map/ppermute | solution.py:19
  34.1 7.5 %collective-permute-done.3 = f32[1,7,1326]{2,1,0:T(8,128)S(1)} collective-permute-done((f32[1,7,1326]{2,1,0:T(8,128)S(1)}, f32[1,7,1326]{2,1,0:T(8,128)S(1)}, u32[]{:S(2)}, u32[]{:S(2)}) %collective-permute-start.3) | collective-permute-done | bytes 37160 | tf_op jit(solution)/shard_map/ppermute | solution.py:19
  43.1 7.5 %collective-permute-done.4 = f32[1,7,1326]{2,1,0:T(8,128)S(1)} collective-permute-done((f32[1,7,1326]{2,1,0:T(8,128)S(1)}, f32[1,7,1326]{2,1,0:T(8,128)S(1)}, u32[]{:S(2)}, u32[]{:S(2)}) %collective-permute-start.4) | collective-permute-done | bytes 37160 | tf_op jit(solution)/shard_map/ppermute | solution.py:19
  52.4 7.5 %collective-permute-done.5 = f32[1,7,1326]{2,1,0:T(8,128)S(1)} collective-permute-done((f32[1,7,1326]{2,1,0:T(8,128)S(1)}, f32[1,7,1326]{2,1,0:T(8,128)S(1)}, u32[]{:S(2)}, u32[]{:S(2)}) %collective-permute-start.5) | collective-permute-done | bytes 37160 | tf_op jit(solution)/shard_map/ppermute | solution.py:19
  62.2 3.7 %fusion.35 = f32[256,1326]{0,1:T(8,128)S(1)} fusion(s32[1326]{0:T(1024)S(1)} %reduce.22, pred[1326]{0:T(1024)(128)(4,1)S(1)} %compare_reduce_fusion, s32[1326]{0:T(1024)S(1)} %copy-done.61, s32[1326]{0:T(1024)S(1)} %copy-done.63, bf16[1,128,1326]{2,1,0:T(8,128)(2,1)S(1)} %get-tuple-element.58, bf16[1,128,1326]{2,1,0:T(8,128)(2,1)S(1)} %get-tuple-element.43), kind=kOutput, calls=%fused_computation.82 | convolution fusion | flops 929727552 | bytes 2053974 | tf_op jit(solution)/shard_map/bij,bnj->bni/dot_general | solution.py:116
  65.9 3.5 %fusion.9 = f32[1,256,1326]{1,2,0:T(8,128)S(1)} fusion(f32[256,1326]{0,1:T(8,128)S(1)} %fusion.35, s32[1326]{0:T(1024)S(1)} %copy-done.61, s32[1326]{0:T(1024)S(1)} %copy-done.63, pred[1326]{0:T(1024)(128)(4,1)S(1)} %compare_reduce_fusion, bf16[1,128,1326]{2,1,0:T(8,128)(2,1)S(1)} %fusion.56, bf16[1,128,1326]{2,1,0:T(8,128)(2,1)S(1)} %get-tuple-element.42), kind=kOutput, calls=%fused_computation.34 | convolution fusion | flops 923033920 | bytes 3406494 | tf_op jit(solution)/shard_map/bij,bnj->bni/dot_general | solution.py:118
  69.5 0.9 fusion.205
  70.4 1.4 copy.20
  72.0 0.8 convolution_bitcast_fusion.9
  72.7 0.9 fusion.92
  73.7 1.1 copy.21
  74.8 1.7 slice_multiply_fusion.3
  76.5 1.0 mul.336
  77.6 1.6 fusion.90
  79.2 1.4 convolution_bitcast_fusion.6
  80.7 1.0 fusion.66
  81.6 1.0 reshape.1792
  82.7 0.9 fusion.84
  83.6 0.8 convolution_bitcast_fusion.8
  84.9 1.2 fusion.29
  86.8 3.7 %collective-permute-start.10 = (f32[1,7,1326]{2,1,0:T(8,128)S(1)}, f32[1,7,1326]{2,1,0:T(8,128)S(1)}, u32[]{:S(2)}, u32[]{:S(2)}) collective-permute-start(f32[1,7,1326]{2,1,0:T(8,128)S(1)} %convolution_bitcast_fusion.5), channel_id=1, source_target_pairs={{0,30},{2,0},{4,2},{6,4},{8,6},{10,8},{12,10},{14,12},{16,14},{18,... | collective-permute-start | bytes 111392 | tf_op jit(solution)/shard_map/ppermute | solution.py:19
  91.3 1.8 collective-permute-start.8
  93.4 2.0 collective-permute-done.8
  95.7 0.8 multiply_reduce_fusion.1
  96.5 40.5 %psum.14 = f32[]{:T(128)} all-reduce(f32[]{:T(128)} %multiply_reduce_fusion.1), channel_id=1, replica_groups=mesh['node'=16,'board'=2] {'node','board'}, use_global_device_ids=true, to_apply=%region_11.14 | all-reduce | flops 1 | bytes 8 | tf_op jit(solution)/shard_map/psum | solution.py:192
  140.2 1.2 exponential_divide_fusion
  141.5 0.7 gather_fusion.12
  142.3 2.3 collective-permute-start.11
  144.6 5.3 %collective-permute-done.11 = f32[1,7,1326]{2,1,0:T(8,128)S(1)} collective-permute-done((f32[1,7,1326]{2,1,0:T(8,128)S(1)}, f32[1,7,1326]{2,1,0:T(8,128)S(1)}, u32[]{:S(2)}, u32[]{:S(2)}) %collective-permute-start.11) | collective-permute-done | bytes 37160 | tf_op jit(solution)/shard_map/ppermute | solution.py:19
  149.9 0.8 gather_fusion.13
  150.9 0.7 gather_fusion.14
  151.7 7.5 %collective-permute-done.12 = f32[1,7,1326]{2,1,0:T(8,128)S(1)} collective-permute-done((f32[1,7,1326]{2,1,0:T(8,128)S(1)}, f32[1,7,1326]{2,1,0:T(8,128)S(1)}, u32[]{:S(2)}, u32[]{:S(2)}) %collective-permute-start.12) | collective-permute-done | bytes 37160 | tf_op jit(solution)/shard_map/ppermute | solution.py:19
  159.3 0.9 gather_fusion.15
  160.3 0.7 gather_fusion.16
  161.2 7.6 %collective-permute-done.13 = f32[1,7,1326]{2,1,0:T(8,128)S(1)} collective-permute-done((f32[1,7,1326]{2,1,0:T(8,128)S(1)}, f32[1,7,1326]{2,1,0:T(8,128)S(1)}, u32[]{:S(2)}, u32[]{:S(2)}) %collective-permute-start.13) | collective-permute-done | bytes 37160 | tf_op jit(solution)/shard_map/ppermute | solution.py:19
  168.8 0.8 gather_fusion.17
  169.6 0.7 gather_fusion.18
  170.5 7.5 %collective-permute-done.14 = f32[1,7,1326]{2,1,0:T(8,128)S(1)} collective-permute-done((f32[1,7,1326]{2,1,0:T(8,128)S(1)}, f32[1,7,1326]{2,1,0:T(8,128)S(1)}, u32[]{:S(2)}, u32[]{:S(2)}) %collective-permute-start.14) | collective-permute-done | bytes 37160 | tf_op jit(solution)/shard_map/ppermute | solution.py:19
  178.1 0.8 gather_fusion.19
  178.9 0.7 gather_fusion.20
  179.8 7.6 %collective-permute-done.15 = f32[1,7,1326]{2,1,0:T(8,128)S(1)} collective-permute-done((f32[1,7,1326]{2,1,0:T(8,128)S(1)}, f32[1,7,1326]{2,1,0:T(8,128)S(1)}, u32[]{:S(2)}, u32[]{:S(2)}) %collective-permute-start.15) | collective-permute-done | bytes 37160 | tf_op jit(solution)/shard_map/ppermute | solution.py:19
  187.4 0.8 gather_fusion.21
  189.5 3.6 %fusion.34 = f32[256,1326]{0,1:T(8,128)S(1)} fusion(s32[1326]{0:T(1024)S(1)} %copy-done.37, pred[1326]{0:T(1024)(128)(4,1)S(1)} %copy-done.60, s32[1326]{0:T(1024)S(1)} %copy-done.62, s32[1326]{0:T(1024)S(1)} %copy-done.64, bf16[1,128,1326]{2,1,0:T(8,128)(2,1)S(1)} %get-tuple-element.59, bf16[1,128,1326]{2,1,0:T(8,128)(2,1)S(1)} %get-tuple-element.37), kind=kOutput, calls=%fused_computation.81 | convolution fusion | flops 929727552 | bytes 2053974 | tf_op jit(solution)/shard_map/bij,bnj->bni/dot_general | solution.py:116
  193.2 3.5 %fusion.8 = f32[1,256,1326]{1,2,0:T(8,128)S(1)} fusion(f32[256,1326]{0,1:T(8,128)S(1)} %fusion.34, s32[1326]{0:T(1024)S(1)} %copy-done.62, s32[1326]{0:T(1024)S(1)} %copy-done.64, pred[1326]{0:T(1024)(128)(4,1)S(1)} %copy-done.60, bf16[1,128,1326]{2,1,0:T(8,128)(2,1)S(1)} %fusion.57, bf16[1,128,1326]{2,1,0:T(8,128)(2,1)S(1)} %get-tuple-element.36), kind=kOutput, calls=%fused_computation.33 | convolution fusion | flops 923033920 | bytes 3406494 | tf_op jit(solution)/shard_map/bij,bnj->bni/dot_general | solution.py:118
  197.5 0.8 convolution_bitcast_fusion.4
  198.6 1.1 copy.23
  199.7 1.6 slice_multiply_fusion.1
  202.0 0.8 collective-permute-done.16
  202.8 0.9 fusion.67
  204.4 3.7 %collective-permute-start.17 = (f32[1,7,1326]{2,1,0:T(8,128)S(1)}, f32[1,7,1326]{2,1,0:T(8,128)S(1)}, u32[]{:S(2)}, u32[]{:S(2)}) collective-permute-start(f32[1,7,1326]{2,1,0:T(8,128)S(1)} %convolution_bitcast_fusion.3), channel_id=1, source_target_pairs={{0,30},{2,0},{4,2},{6,4},{8,6},{10,8},{12,10},{14,12},{16,14},{18,... | collective-permute-start | bytes 111392 | tf_op jit(solution)/shard_map/ppermute | solution.py:19
  208.1 1.1 fusion.22
  209.8 1.7 collective-permute-start.20
  212.5 4.2 %collective-permute-start.18 = (f32[1,7,1326]{2,1,0:T(8,128)S(1)}, f32[1,7,1326]{2,1,0:T(8,128)S(1)}, u32[]{:S(2)}, u32[]{:S(2)}) collective-permute-start(f32[1,7,1326]{2,1,0:T(8,128)S(1)} %convolution_bitcast_fusion.2), channel_id=1, source_target_pairs={{0,30},{2,0},{4,2},{6,4},{8,6},{10,8},{12,10},{14,12},{16,14},{18,... | collective-permute-start | bytes 111392 | tf_op jit(solution)/shard_map/ppermute | solution.py:19
  217.0 1.4 collective-permute-done.18
  218.7 0.8 multiply_reduce_fusion
  219.5 40.5 %psum.15 = f32[]{:T(128)} all-reduce(f32[]{:T(128)} %get-tuple-element.10), channel_id=1, replica_groups=mesh['node'=16,'board'=2] {'node','board'}, use_global_device_ids=true, to_apply=%region_20.23 | all-reduce | flops 1 | bytes 8 | tf_op jit(solution)/shard_map/psum | solution.py:192
  260.8 1.0 multiply_add_fusion
  (312 shorter events, 28.5 us)
Async XLA Ops:
  0.6 7.4 %copy-start = (f32[1,4,32,1326]{3,2,1,0:T(8,128)S(1)}, f32[1,4,32,1326]{3,2,1,0:T(8,128)}, u32[]{:S(2)}) copy-start(f32[1,4,32,1326]{3,2,1,0:T(8,128)} %param.14) | copy-start | bytes 2036740
  2.3 31.6 %copy-start.44 = (pred[7]{0:T(512)(128)(4,1)}, pred[7]{0:T(512)(128)(4,1)S(1)}, u32[]{:S(2)}) copy-start(pred[7]{0:T(512)(128)(4,1)S(1)} %get-tuple-element.28) | copy-start | bytes 25
  2.3 31.0 %copy-start.38 = (s32[1024]{0:T(1024)}, s32[1024]{0:T(1024)S(1)}, u32[]{:S(2)}) copy-start(s32[1024]{0:T(1024)S(1)} %pad_clamp_fusion.5) | copy-start | bytes 12292
  3.7 10.7 %collective-permute-start = (f32[1,7,1326]{2,1,0:T(8,128)S(1)}, f32[1,7,1326]{2,1,0:T(8,128)S(1)}, u32[]{:S(2)}, u32[]{:S(2)}) collective-permute-start(f32[1,7,1326]{2,1,0:T(8,128)S(1)} %bitcast_select_fusion.21), channel_id=1, source_target_pairs={{0,2},{2,4},{4,6},{6,8},{8,10},{10,12},{12,14},{14,16},{16,18},{18... | collective-permute-start | bytes 111392 | tf_op jit(solution)/shard_map/ppermute | solution.py:19
  6.7 5.2 %copy-start.41 = (f32[1,1326]{1,0:T(1,128)S(1)}, f32[1,1326]{1,0:T(1,128)}, u32[]{:S(2)}) copy-start(f32[1,1326]{1,0:T(1,128)} %param.18) | copy-start | bytes 15916
  8.3 57.6 %copy-start.59 = (pred[1326]{0:T(1024)(128)(4,1)}, pred[1326]{0:T(1024)(128)(4,1)S(1)}, u32[]{:S(2)}) copy-start(pred[1326]{0:T(1024)(128)(4,1)S(1)} %compare_reduce_fusion) | copy-start | bytes 3982
  8.6 34.3 %copy-start.34 = (pred[7]{0:T(512)(128)(4,1)}, pred[7]{0:T(512)(128)(4,1)S(1)}, u32[]{:S(2)}) copy-start(pred[7]{0:T(512)(128)(4,1)S(1)} %get-tuple-element.24) | copy-start | bytes 25
  8.9 43.1 %copy-start.32 = (pred[7]{0:T(512)(128)(4,1)}, pred[7]{0:T(512)(128)(4,1)S(1)}, u32[]{:S(2)}) copy-start(pred[7]{0:T(512)(128)(4,1)S(1)} %get-tuple-element.20) | copy-start | bytes 25
  9.0 51.0 %copy-start.14 = (s32[1024]{0:T(1024)}, s32[1024]{0:T(1024)S(1)}, u32[]{:S(2)}) copy-start(s32[1024]{0:T(1024)S(1)} %pad_clamp_fusion) | copy-start | bytes 12292
  9.0 42.4 %copy-start.15 = (s32[1024]{0:T(1024)}, s32[1024]{0:T(1024)S(1)}, u32[]{:S(2)}) copy-start(s32[1024]{0:T(1024)S(1)} %pad_clamp_fusion.1) | copy-start | bytes 12292
  9.0 33.3 %copy-start.17 = (s32[1024]{0:T(1024)}, s32[1024]{0:T(1024)S(1)}, u32[]{:S(2)}) copy-start(s32[1024]{0:T(1024)S(1)} %pad_clamp_fusion.3) | copy-start | bytes 12292
  9.1 41.6 %copy-start.16 = (s32[1024]{0:T(1024)}, s32[1024]{0:T(1024)S(1)}, u32[]{:S(2)}) copy-start(s32[1024]{0:T(1024)S(1)} %pad_clamp_fusion.2) | copy-start | bytes 12292
  9.2 32.5 %copy-start.39 = (s32[1024]{0:T(1024)}, s32[1024]{0:T(1024)S(1)}, u32[]{:S(2)}) copy-start(s32[1024]{0:T(1024)S(1)} %pad_clamp_fusion.4) | copy-start | bytes 12292
  11.8 60.1 %copy-start.25 = (pred[8]{0:T(512)(128)(4,1)}, pred[8]{0:T(512)(128)(4,1)S(1)}, u32[]{:S(2)}) copy-start(pred[8]{0:T(512)(128)(4,1)S(1)} %get-tuple-element.16) | copy-start | bytes 28
  11.8 60.9 %copy-start.27 = (s32[8]{0:T(128)}, s32[8]{0:T(128)S(1)}, u32[]{:S(2)}) copy-start(s32[8]{0:T(128)S(1)} %get-tuple-element.17) | copy-start | bytes 100
  11.9 60.1 %copy-start.29 = (s32[8]{0:T(128)}, s32[8]{0:T(128)S(1)}, u32[]{:S(2)}) copy-start(s32[8]{0:T(128)S(1)} %fusion.189) | copy-start | bytes 100
  14.5 3.1 %copy-start.42 = (s32[1,1326]{1,0:T(1,128)S(1)}, s32[1,1326]{1,0:T(1,128)}, u32[]{:S(2)}) copy-start(s32[1,1326]{1,0:T(1,128)} %param.20) | copy-start | bytes 15916
  15.1 2.4 copy-start.5
  15.9 7.6 %collective-permute-start.1 = (f32[1,7,1326]{2,1,0:T(8,128)S(1)}, f32[1,7,1326]{2,1,0:T(8,128)S(1)}, u32[]{:S(2)}, u32[]{:S(2)}) collective-permute-start(f32[1,7,1326]{2,1,0:T(8,128)S(1)} %bitcast_select_fusion.20), channel_id=1, source_target_pairs={{0,2},{2,4},{4,6},{6,8},{8,10},{10,12},{12,14},{14,16},{16,18},{18... | collective-permute-start | bytes 111392 | tf_op jit(solution)/shard_map/ppermute | solution.py:19
  17.5 44.0 %copy-start.46 = (f32[128]{0:T(128)}, f32[128]{0:T(128)S(1)}, u32[]{:S(2)}) copy-start(f32[128]{0:T(128)S(1)} %mul.319) | copy-start | bytes 1540
  17.6 44.2 %copy-start.36 = (s32[1326]{0:T(1024)}, s32[1326]{0:T(1024)S(1)}, u32[]{:S(2)}) copy-start(s32[1326]{0:T(1024)S(1)} %reduce.22) | copy-start | bytes 15916
  24.9 7.6 %collective-permute-start.2 = (f32[1,7,1326]{2,1,0:T(8,128)S(1)}, f32[1,7,1326]{2,1,0:T(8,128)S(1)}, u32[]{:S(2)}, u32[]{:S(2)}) collective-permute-start(f32[1,7,1326]{2,1,0:T(8,128)S(1)} %bitcast_select_fusion.19), channel_id=1, source_target_pairs={{0,2},{2,4},{4,6},{6,8},{8,10},{10,12},{12,14},{14,16},{16,18},{18... | collective-permute-start | bytes 111392 | tf_op jit(solution)/shard_map/ppermute | solution.py:19
  34.0 7.6 %collective-permute-start.3 = (f32[1,7,1326]{2,1,0:T(8,128)S(1)}, f32[1,7,1326]{2,1,0:T(8,128)S(1)}, u32[]{:S(2)}, u32[]{:S(2)}) collective-permute-start(f32[1,7,1326]{2,1,0:T(8,128)S(1)} %bitcast_select_fusion.18), channel_id=1, source_target_pairs={{0,2},{2,4},{4,6},{6,8},{8,10},{10,12},{12,14},{14,16},{16,18},{18... | collective-permute-start | bytes 111392 | tf_op jit(solution)/shard_map/ppermute | solution.py:19
  43.0 7.6 %collective-permute-start.4 = (f32[1,7,1326]{2,1,0:T(8,128)S(1)}, f32[1,7,1326]{2,1,0:T(8,128)S(1)}, u32[]{:S(2)}, u32[]{:S(2)}) collective-permute-start(f32[1,7,1326]{2,1,0:T(8,128)S(1)} %bitcast_select_fusion.17), channel_id=1, source_target_pairs={{0,2},{2,4},{4,6},{6,8},{8,10},{10,12},{12,14},{14,16},{16,18},{18... | collective-permute-start | bytes 111392 | tf_op jit(solution)/shard_map/ppermute | solution.py:19
  52.1 7.8 %collective-permute-start.5 = (f32[1,7,1326]{2,1,0:T(8,128)S(1)}, f32[1,7,1326]{2,1,0:T(8,128)S(1)}, u32[]{:S(2)}, u32[]{:S(2)}) collective-permute-start(f32[1,7,1326]{2,1,0:T(8,128)S(1)} %bitcast_select_fusion.16), channel_id=1, source_target_pairs={{0,2},{2,4},{4,6},{6,8},{8,10},{10,12},{12,14},{14,16},{16,18},{18... | collective-permute-start | bytes 111392 | tf_op jit(solution)/shard_map/ppermute | solution.py:19
  72.7 7.9 %collective-permute-start.6 = (f32[1,7,1326]{2,1,0:T(8,128)}, f32[1,7,1326]{2,1,0:T(8,128)S(1)}, u32[]{:S(2)}, u32[]{:S(2)}) collective-permute-start(f32[1,7,1326]{2,1,0:T(8,128)} %convolution_bitcast_fusion.9), channel_id=1, source_target_pairs={{0,30},{2,0},{4,2},{6,4},{8,6},{10,8},{12,10},{14,12},{16,14},{18,... | collective-permute-start | bytes 111392 | tf_op jit(solution)/shard_map/ppermute | solution.py:19
  74.8 5.8 %copy-start.9 = (f32[1326,32]{0,1:T(8,128)S(1)}, f32[1326,32]{0,1:T(8,128)}, u32[]{:S(2)}) copy-start(f32[1326,32]{0,1:T(8,128)} %fusion.92) | copy-start | bytes 509188
  76.5 8.4 %copy-start.4 = (f32[1,128,1326]{2,1,0:T(8,128)S(1)}, f32[1,128,1326]{2,1,0:T(8,128)}, u32[]{:S(2)}) copy-start(f32[1,128,1326]{2,1,0:T(8,128)} %copy.21) | copy-start | bytes 2036740
  80.6 4.3 %collective-permute-start.9 = (f32[1,7,1326]{2,1,0:T(8,128)}, f32[1,7,1326]{2,1,0:T(8,128)S(1)}, u32[]{:S(2)}, u32[]{:S(2)}) collective-permute-start(f32[1,7,1326]{2,1,0:T(8,128)} %convolution_bitcast_fusion.6), channel_id=1, source_target_pairs={{0,30},{2,0},{4,2},{6,4},{8,6},{10,8},{12,10},{14,12},{16,14},{18,... | collective-permute-start | bytes 111392 | tf_op jit(solution)/shard_map/ppermute | solution.py:19
  81.6 4.7 %copy-start.21 = (s32[8]{0:T(128)S(1)}, s32[8]{0:T(128)}, u32[]{:S(2)}) copy-start(s32[8]{0:T(128)} %copy-done.20) | copy-start | bytes 100
  81.6 5.0 %copy-start.18 = (pred[8]{0:T(512)(128)(4,1)S(1)}, pred[8]{0:T(512)(128)(4,1)}, u32[]{:S(2)}) copy-start(pred[8]{0:T(512)(128)(4,1)} %get-tuple-element.14) | copy-start | bytes 28
  81.6 5.0 %copy-start.23 = (s32[8]{0:T(128)S(1)}, s32[8]{0:T(128)}, u32[]{:S(2)}) copy-start(s32[8]{0:T(128)} %fusion.188) | copy-start | bytes 100
  81.6 8.8 %copy-start.12 = (pred[32]{0:T(512)(128)(4,1)S(1)}, pred[32]{0:T(512)(128)(4,1)}, u32[]{:S(2)}) copy-start(pred[32]{0:T(512)(128)(4,1)} %get-tuple-element.53) | copy-start | bytes 100
  83.6 7.3 %copy-start.56 = (s32[8]{0:T(128)S(1)}, s32[8]{0:T(128)}, u32[]{:S(2)}) copy-start(s32[8]{0:T(128)} %copy-done.55) | copy-start | bytes 100
  84.4 6.7 %copy-start.51 = (pred[8]{0:T(512)(128)(4,1)S(1)}, pred[8]{0:T(512)(128)(4,1)}, u32[]{:S(2)}) copy-start(pred[8]{0:T(512)(128)(4,1)} %get-tuple-element.12) | copy-start | bytes 28
  84.5 6.7 %copy-start.53 = (s32[8]{0:T(128)S(1)}, s32[8]{0:T(128)}, u32[]{:S(2)}) copy-start(s32[8]{0:T(128)} %fusion.187) | copy-start | bytes 100
  84.5 5.9 %collective-permute-start.7 = (f32[1,7,1326]{2,1,0:T(8,128)S(1)}, f32[1,7,1326]{2,1,0:T(8,128)S(1)}, u32[]{:S(2)}, u32[]{:S(2)}) collective-permute-start(f32[1,7,1326]{2,1,0:T(8,128)S(1)} %convolution_bitcast_fusion.8), channel_id=1, source_target_pairs={{0,30},{2,0},{4,2},{6,4},{8,6},{10,8},{12,10},{14,12},{16,14},{18,... | collective-permute-start | bytes 111392 | tf_op jit(solution)/shard_map/ppermute | solution.py:19
  86.2 9.3 %copy-start.49 = (pred[32]{0:T(512)(128)(4,1)S(1)}, pred[32]{0:T(512)(128)(4,1)}, u32[]{:S(2)}) copy-start(pred[32]{0:T(512)(128)(4,1)} %get-tuple-element.48) | copy-start | bytes 100
  86.8 6.4 %collective-permute-start.10 = (f32[1,7,1326]{2,1,0:T(8,128)S(1)}, f32[1,7,1326]{2,1,0:T(8,128)S(1)}, u32[]{:S(2)}, u32[]{:S(2)}) collective-permute-start(f32[1,7,1326]{2,1,0:T(8,128)S(1)} %convolution_bitcast_fusion.5), channel_id=1, source_target_pairs={{0,30},{2,0},{4,2},{6,4},{8,6},{10,8},{12,10},{14,12},{16,14},{18,... | collective-permute-start | bytes 111392 | tf_op jit(solution)/shard_map/ppermute | solution.py:19
  91.3 4.1 %collective-permute-start.8 = (f32[1,7,1326]{2,1,0:T(8,128)S(1)}, f32[1,7,1326]{2,1,0:T(8,128)S(1)}, u32[]{:S(2)}, u32[]{:S(2)}) collective-permute-start(f32[1,7,1326]{2,1,0:T(8,128)S(1)} %convolution_bitcast_fusion.7), channel_id=1, source_target_pairs={{0,30},{2,0},{4,2},{6,4},{8,6},{10,8},{12,10},{14,12},{16,14},{18,... | collective-permute-start | bytes 111392 | tf_op jit(solution)/shard_map/ppermute | solution.py:19
  95.7 42.0 %copy-start.2 = (f32[1,1,32,1326]{3,2,1,0:T(8,128)}, f32[1,1,32,1326]{3,2,1,0:T(8,128)S(1)}, u32[]{:S(2)}) copy-start(f32[1,1,32,1326]{3,2,1,0:T(8,128)S(1)} %fusion.31) | copy-start | bytes 509188
  142.3 7.6 %collective-permute-start.11 = (f32[1,7,1326]{2,1,0:T(8,128)S(1)}, f32[1,7,1326]{2,1,0:T(8,128)S(1)}, u32[]{:S(2)}, u32[]{:S(2)}) collective-permute-start(f32[1,7,1326]{2,1,0:T(8,128)S(1)} %bitcast_select_fusion.15), channel_id=1, source_target_pairs={{0,2},{2,4},{4,6},{6,8},{8,10},{10,12},{12,14},{14,16},{16,18},{18... | collective-permute-start | bytes 111392 | tf_op jit(solution)/shard_map/ppermute | solution.py:19
  151.7 7.6 %collective-permute-start.12 = (f32[1,7,1326]{2,1,0:T(8,128)S(1)}, f32[1,7,1326]{2,1,0:T(8,128)S(1)}, u32[]{:S(2)}, u32[]{:S(2)}) collective-permute-start(f32[1,7,1326]{2,1,0:T(8,128)S(1)} %bitcast_select_fusion.14), channel_id=1, source_target_pairs={{0,2},{2,4},{4,6},{6,8},{8,10},{10,12},{12,14},{14,16},{16,18},{18... | collective-permute-start | bytes 111392 | tf_op jit(solution)/shard_map/ppermute | solution.py:19
  161.1 7.6 %collective-permute-start.13 = (f32[1,7,1326]{2,1,0:T(8,128)S(1)}, f32[1,7,1326]{2,1,0:T(8,128)S(1)}, u32[]{:S(2)}, u32[]{:S(2)}) collective-permute-start(f32[1,7,1326]{2,1,0:T(8,128)S(1)} %bitcast_select_fusion.13), channel_id=1, source_target_pairs={{0,2},{2,4},{4,6},{6,8},{8,10},{10,12},{12,14},{14,16},{16,18},{18... | collective-permute-start | bytes 111392 | tf_op jit(solution)/shard_map/ppermute | solution.py:19
  170.4 7.6 %collective-permute-start.14 = (f32[1,7,1326]{2,1,0:T(8,128)S(1)}, f32[1,7,1326]{2,1,0:T(8,128)S(1)}, u32[]{:S(2)}, u32[]{:S(2)}) collective-permute-start(f32[1,7,1326]{2,1,0:T(8,128)S(1)} %bitcast_select_fusion.12), channel_id=1, source_target_pairs={{0,2},{2,4},{4,6},{6,8},{8,10},{10,12},{12,14},{14,16},{16,18},{18... | collective-permute-start | bytes 111392 | tf_op jit(solution)/shard_map/ppermute | solution.py:19
  179.7 7.7 %collective-permute-start.15 = (f32[1,7,1326]{2,1,0:T(8,128)S(1)}, f32[1,7,1326]{2,1,0:T(8,128)S(1)}, u32[]{:S(2)}, u32[]{:S(2)}) collective-permute-start(f32[1,7,1326]{2,1,0:T(8,128)S(1)} %bitcast_select_fusion.11), channel_id=1, source_target_pairs={{0,2},{2,4},{4,6},{6,8},{8,10},{10,12},{12,14},{14,16},{16,18},{18... | collective-permute-start | bytes 111392 | tf_op jit(solution)/shard_map/ppermute | solution.py:19
  198.5 4.3 %collective-permute-start.16 = (f32[1,7,1326]{2,1,0:T(8,128)}, f32[1,7,1326]{2,1,0:T(8,128)S(1)}, u32[]{:S(2)}, u32[]{:S(2)}) collective-permute-start(f32[1,7,1326]{2,1,0:T(8,128)} %convolution_bitcast_fusion.4), channel_id=1, source_target_pairs={{0,30},{2,0},{4,2},{6,4},{8,6},{10,8},{12,10},{14,12},{16,14},{18,... | collective-permute-start | bytes 111392 | tf_op jit(solution)/shard_map/ppermute | solution.py:19
  198.6 3.2 %copy-start.31 = (s32[8]{0:T(128)S(1)}, s32[8]{0:T(128)}, u32[]{:S(2)}) copy-start(s32[8]{0:T(128)} %copy-done.29) | copy-start | bytes 100
  201.3 2.6 copy-start.22
  201.3 2.9 %copy-start.19 = (pred[8]{0:T(512)(128)(4,1)S(1)}, pred[8]{0:T(512)(128)(4,1)}, u32[]{:S(2)}) copy-start(pred[8]{0:T(512)(128)(4,1)} %get-tuple-element.14) | copy-start | bytes 28
  201.4 2.9 %copy-start.24 = (s32[8]{0:T(128)S(1)}, s32[8]{0:T(128)}, u32[]{:S(2)}) copy-start(s32[8]{0:T(128)} %fusion.188) | copy-start | bytes 100
  201.4 6.7 %copy-start.3 = (f32[1,128,1326]{2,1,0:T(8,128)S(1)}, f32[1,128,1326]{2,1,0:T(8,128)}, u32[]{:S(2)}) copy-start(f32[1,128,1326]{2,1,0:T(8,128)} %copy.23) | copy-start | bytes 2036740
  202.0 6.1 %collective-permute-start.19 = (f32[1,7,1326]{2,1,0:T(8,128)S(1)}, f32[1,7,1326]{2,1,0:T(8,128)}, u32[]{:S(2)}, u32[]{:S(2)}) collective-permute-start(f32[1,7,1326]{2,1,0:T(8,128)S(1)} %convolution_bitcast_fusion.1), channel_id=1, source_target_pairs={{0,30},{2,0},{4,2},{6,4},{8,6},{10,8},{12,10},{14,12},{16,14},{18,... | collective-permute-start | bytes 111392 | tf_op jit(solution)/shard_map/ppermute | solution.py:19
  203.8 7.8 %copy-start.13 = (pred[32]{0:T(512)(128)(4,1)S(1)}, pred[32]{0:T(512)(128)(4,1)}, u32[]{:S(2)}) copy-start(pred[32]{0:T(512)(128)(4,1)} %get-tuple-element.53) | copy-start | bytes 100
  204.3 7.7 %copy-start.57 = (s32[8]{0:T(128)S(1)}, s32[8]{0:T(128)}, u32[]{:S(2)}) copy-start(s32[8]{0:T(128)} %copy-done.55) | copy-start | bytes 100
  204.4 7.9 %copy-start.52 = (pred[8]{0:T(512)(128)(4,1)S(1)}, pred[8]{0:T(512)(128)(4,1)}, u32[]{:S(2)}) copy-start(pred[8]{0:T(512)(128)(4,1)} %get-tuple-element.12) | copy-start | bytes 28
  204.4 7.9 %copy-start.54 = (s32[8]{0:T(128)S(1)}, s32[8]{0:T(128)}, u32[]{:S(2)}) copy-start(s32[8]{0:T(128)} %fusion.187) | copy-start | bytes 100
  204.4 7.1 %collective-permute-start.17 = (f32[1,7,1326]{2,1,0:T(8,128)S(1)}, f32[1,7,1326]{2,1,0:T(8,128)S(1)}, u32[]{:S(2)}, u32[]{:S(2)}) collective-permute-start(f32[1,7,1326]{2,1,0:T(8,128)S(1)} %convolution_bitcast_fusion.3), channel_id=1, source_target_pairs={{0,30},{2,0},{4,2},{6,4},{8,6},{10,8},{12,10},{14,12},{16,14},{18,... | collective-permute-start | bytes 111392 | tf_op jit(solution)/shard_map/ppermute | solution.py:19
  209.2 9.2 %copy-start.50 = (pred[32]{0:T(512)(128)(4,1)S(1)}, pred[32]{0:T(512)(128)(4,1)}, u32[]{:S(2)}) copy-start(pred[32]{0:T(512)(128)(4,1)} %get-tuple-element.48) | copy-start | bytes 100
  209.6 9.1 %copy-start.10 = (f32[1,1,32,1326]{3,2,1,0:T(8,128)S(1)}, f32[1,1,32,1326]{3,2,1,0:T(8,128)}, u32[]{:S(2)}) copy-start(f32[1,1,32,1326]{3,2,1,0:T(8,128)} %get-tuple-element.35) | copy-start | bytes 509188
  209.7 9.1 %copy-start.11 = (f32[1,32,1326]{2,1,0:T(8,128)S(1)}, f32[1,32,1326]{2,1,0:T(8,128)}, u32[]{:S(2)}) copy-start(f32[1,32,1326]{2,1,0:T(8,128)} %get-tuple-element.63) | copy-start | bytes 509188
  209.8 6.9 %collective-permute-start.20 = (f32[1,7,1326]{2,1,0:T(8,128)S(1)}, f32[1,7,1326]{2,1,0:T(8,128)S(1)}, u32[]{:S(2)}, u32[]{:S(2)}) collective-permute-start(f32[1,7,1326]{2,1,0:T(8,128)S(1)} %convolution_bitcast_fusion), channel_id=1, source_target_pairs={{0,30},{2,0},{4,2},{6,4},{8,6},{10,8},{12,10},{14,12},{16,14},{18,... | collective-permute-start | bytes 111392 | tf_op jit(solution)/shard_map/ppermute | solution.py:19
  212.5 6.0 %collective-permute-start.18 = (f32[1,7,1326]{2,1,0:T(8,128)S(1)}, f32[1,7,1326]{2,1,0:T(8,128)S(1)}, u32[]{:S(2)}, u32[]{:S(2)}) collective-permute-start(f32[1,7,1326]{2,1,0:T(8,128)S(1)} %convolution_bitcast_fusion.2), channel_id=1, source_target_pairs={{0,30},{2,0},{4,2},{6,4},{8,6},{10,8},{12,10},{14,12},{16,14},{18,... | collective-permute-start | bytes 111392 | tf_op jit(solution)/shard_map/ppermute | solution.py:19
  219.5 42.2 %copy-start.1 = (f32[1,4,32,1326]{3,2,1,0:T(8,128)}, f32[1,4,32,1326]{3,2,1,0:T(8,128)S(1)}, u32[]{:S(2)}) copy-start(f32[1,4,32,1326]{3,2,1,0:T(8,128)S(1)} %get-tuple-element.11) | copy-start | bytes 2036740
  (22 other events, 22.4 us)
where the time goes:
time: 263 us; the launch traced here: 262 us
  blocking collectives  81.1 us (31%)
  waiting for transfers between devices  76.3 us (29%)
  matrix products  30.1 us (11%)
  local copies, waits for them, and re-layouts  28.7 us (11%)
  starting transfers between devices  22.2 us (8%)
  other arithmetic  19.7 us (7%)
  between operations  3.67 us (1%)
    psum x2, blocking collectives, rate_for(): lax.psum(jnp.sum(values_found * values_found), ('node', 'board'))  81.1 us
    ppermute x21, waiting for transfers between devices, passed_along(): return lax.ppermute(value, axis, pairs)  76.3 us
    ppermute x21, starting transfers between devices, passed_along(): return lax.ppermute(value, axis, pairs)  22.2 us
    dot_general x2, matrix products, terminal_pay(): jnp.einsum('bij,bnj->bni', show_block, show_cols, preferred_element_type=...  7.3 us
    dot_general x2, matrix products, terminal_pay(): jnp.einsum('bij,bnj->bni', compat_block, fold_cols, preferred_element_typ...  7.08 us
  transfers between devices with their start and end apart: 21, of which 14 were waited for; matrix products, arithmetic and copies ran while one was open for 11% of the time, Pallas kernels for 0%

commit v1 on v0

v1 whole, which is shorter than its diff:
```python
import functools

import jax
import jax.numpy as jnp
import numpy as np
from jax import lax
from jax.experimental import pallas as pl
from jax.experimental.pallas import tpu as pltpu
from jax.sharding import PartitionSpec as P

LANES = 128
CARDS = 52
step_scale = 0.5
eps_value = 1e-06
MEBI = 1 << 20


def padded(count):
    return -(-count // LANES) * LANES


def passed_along(value, axis, steps):
    count = lax.axis_size(axis)
    pairs = [(source, (source + steps) % count) for source in range(count)]
    return lax.ppermute(value, axis, pairs)


def card_rows(hand_count, wide):
    pairs = [(low, high) for low in range(CARDS) for high in range(low + 1, CARDS)]
    rows = np.full((2, wide), -1, np.int32)
    rows[:, :hand_count] = np.array(pairs[:hand_count], np.int32).T
    return rows


def payoff_kernel(hands, cards_ref, rank_ref, live_ref, out_ref, flat, left, right):
    wide = out_ref.shape[1]
    flat[...] = jnp.zeros(flat.shape, jnp.float32)
    flat[0:1, 0:hands] = rank_ref[...].astype(jnp.float32)
    flat[1:2, 0:hands] = (live_ref[...] > 0).astype(jnp.float32)
    dead = 1.0 - flat[1:2, :]
    feature = lax.broadcasted_iota(jnp.int32, (LANES, wide), 0)
    hit = (feature == cards_ref[0:1, :]) | (feature == cards_ref[1:2, :])
    base = jnp.where(hit, 1.0, 0.0)
    left[...] = jnp.where(feature == CARDS, dead, jnp.where(feature == CARDS + 1, 1.0, base))
    right[...] = jnp.where(
        feature == CARDS, 1.0, jnp.where(feature == CARDS + 1, dead, base)
    ).astype(jnp.bfloat16)
    rank_row = flat[0:1, :]
    for block in range(wide // LANES):
        part = slice(block * LANES, (block + 1) * LANES)
        left_block = left[:, part].T.astype(jnp.bfloat16)
        rank_col = jnp.broadcast_to(flat[0:1, part], (LANES, LANES)).T[:, 0:1]
        hits = jnp.dot(left_block, right[...], preferred_element_type=jnp.float32)
        compat = jnp.where(hits == 0.0, 1.0, 0.0)
        order = jnp.clip(rank_row - rank_col, -1.0, 1.0)
        out_ref[part, :] = (order * compat).astype(jnp.bfloat16)
        out_ref[wide + block * LANES : wide + (block + 1) * LANES, :] = compat.astype(jnp.bfloat16)


def payoff_blocks(hand_rank, live_mask):
    hands = hand_rank.shape[-1]
    wide = padded(hands)
    return pl.pallas_call(
        functools.partial(payoff_kernel, hands),
        out_shape=jax.ShapeDtypeStruct((2 * wide, wide), jnp.bfloat16),
        scratch_shapes=[
            pltpu.VMEM((8, wide), jnp.float32),
            pltpu.VMEM((LANES, wide), jnp.float32),
            pltpu.VMEM((LANES, wide), jnp.bfloat16),
        ],
        compiler_params=pltpu.CompilerParams(vmem_limit_bytes=20 * MEBI),
        cost_estimate=pl.CostEstimate(
            flops=2 * wide * wide * LANES, bytes_accessed=4 * wide * wide, transcendentals=0
        ),
        name="payoff",
    )(jnp.asarray(card_rows(hands, wide)), hand_rank, live_mask)


def pack_kernel(logits_ref, pot_ref, kind_ref, home_ref, right_ref, left_ref, far_ref, flat):
    levels, tiles, slots, _ = home_ref.shape
    hands = logits_ref.shape[-1]
    pot = pot_ref[...]
    kind = kind_ref[...]
    level = lax.broadcasted_iota(jnp.int32, pot.shape, 0)
    sign = jnp.where(level % 2 == 0, -1.0, 1.0)
    flat[...] = jnp.zeros(flat.shape, jnp.float32)
    flat[0:levels, 0:slots] = jnp.where(kind == 2, pot, 0.0)
    flat[levels : 2 * levels, 0:slots] = jnp.where(kind == 1, pot, 0.0) * sign
    turned = flat[...].T
    lane = lax.broadcasted_iota(jnp.int32, (slots, LANES), 1)
    for idx in range(levels):
        show = turned[0:slots, idx : idx + 1]
        fold = turned[0:slots, levels + idx : levels + idx + 1]
        home_ref[idx, tiles - 1] = jnp.where(
            lane == LANES - 2, show, jnp.where(lane == LANES - 1, fold, 0.0)
        )
        for tile in range(tiles):
            start = tile * LANES
            stop = min(start + LANES, hands)
            home_ref[idx, tile, :, 0 : stop - start] = logits_ref[0, idx, :, start:stop]
    right_ref[...] = home_ref[0]
    left_ref[...] = home_ref[2:4]
    far_ref[...] = home_ref[3, :, 0 : slots - 8, :]


def message_shapes(levels, slots, wide):
    tiles = wide // LANES
    return (
        jax.ShapeDtypeStruct((levels, tiles, slots, LANES), jnp.float32),
        jax.ShapeDtypeStruct((tiles, slots, LANES), jnp.float32),
        jax.ShapeDtypeStruct((2, tiles, slots, LANES), jnp.float32),
        jax.ShapeDtypeStruct((tiles, slots - 8, LANES), jnp.float32),
    )


def packed_rows(logits, pot_size, node_type):
    _, levels, slots, hands = logits.shape
    return pl.pallas_call(
        pack_kernel,
        out_shape=message_shapes(levels, slots, padded(hands)),
        scratch_shapes=[pltpu.VMEM((LANES, LANES), jnp.float32)],
        compiler_params=pltpu.CompilerParams(vmem_limit_bytes=10 * MEBI),
        name="pack",
    )(logits, pot_size, node_type)


def level_offsets(parent_ref, node_count, slots):
    groups = slots // 4
    total = groups * node_count
    first = lax.axis_index("node") * groups
    return [lax.rem(first - parent_ref[idx, 0] // 4 + total, total) for idx in (1, 2, 3)]


def inner_sum(inner, rows):
    total = jnp.where(inner[0], rows[0], 0.0)
    for idx in range(1, 4):
        total = total + jnp.where(inner[idx], rows[idx], 0.0)
    return total


def softmax_four(rows):
    top = jnp.maximum(jnp.maximum(rows[0], rows[1]), jnp.maximum(rows[2], rows[3]))
    lifted = [jnp.exp(row - top) for row in rows]
    total = (lifted[0] + lifted[1]) + (lifted[2] + lifted[3])
    return [row / total for row in lifted]


def operator_q(point, show, fold, range_one, range_two, block_ref, cols, pay):
    wide = block_ref.shape[1]
    inner = [
        [(show[idx][slot] == 0.0) & (fold[idx][slot] == 0.0) for slot in range(4)]
        for idx in range(4)
    ]
    strategy = [softmax_four(point[idx]) for idx in range(4)]
    top_one = [range_one * row for row in strategy[0]]
    above_one = inner_sum(inner[0], top_one)
    mid_two = [range_two * row for row in strategy[1]]
    above_two = inner_sum(inner[1], mid_two)
    low_one = [above_one * row for row in strategy[2]]
    last_one = inner_sum(inner[2], low_one)
    end_two = [above_two * row for row in strategy[3]]
    wide_two = jnp.broadcast_to(range_two, above_two.shape)
    reach_rows = [
        (0, [wide_two] * 4, 1.0),
        (1, mid_two, 1.0),
        (2, [above_two] * 4, 1.0),
        (3, end_two, 1.0),
        (1, [above_one] * 4, -1.0),
        (2, low_one, -1.0),
        (3, [last_one] * 4, -1.0),
    ]
    for unit, (idx, rows, fold_sign) in enumerate(reach_rows):
        for half in range(2):
            place = slice(unit * 32 + half * 16, unit * 32 + half * 16 + 16)
            pair = (2 * half, 2 * half + 1)
            cols[place, 0:wide] = jnp.concatenate(
                [rows[slot] * show[idx][slot] for slot in pair], axis=0
            ).astype(jnp.bfloat16)
            cols[place, wide : 2 * wide] = jnp.concatenate(
                [rows[slot] * (fold[idx][slot] * fold_sign) for slot in pair], axis=0
            ).astype(jnp.bfloat16)
    for start in range(0, wide, 2 * LANES):
        stop = min(start + 2 * LANES, wide)
        pay[:, start:stop] = jnp.dot(
            cols[...], block_ref[:, start:stop], preferred_element_type=jnp.float32
        )

    def paid(unit):
        return [pay[unit * 32 + slot * 8 : unit * 32 + slot * 8 + 8, :] for slot in range(4)]

    def added(rows):
        return (rows[0] + rows[1]) + (rows[2] + rows[3])

    def landed(rows, kept, term):
        return [rows[slot] + jnp.where(kept[slot], term, 0.0) for slot in range(4)]

    value_two_end = paid(6)
    term_two = added([strategy[3][slot] * value_two_end[slot] for slot in range(4)])
    term_two = added(landed(paid(5), inner[2], term_two))
    value_two_mid = landed(paid(4), inner[1], term_two)
    value_one_low = landed(paid(2), inner[2], added(paid(3)))
    term_one = added([strategy[2][slot] * value_one_low[slot] for slot in range(4)])
    term_one = added(landed(paid(1), inner[1], term_one))
    value_one_top = landed(paid(0), inner[0], term_one)
    return [value_one_top, value_two_mid, value_one_low, value_two_end]


def squares(found):
    total = None
    for rows in found:
        for row in rows:
            total = row * row if total is None else total + row * row
    return jnp.broadcast_to(jnp.sum(total), (1, LANES))


def scale_columns(rows):
    wide = rows[0][0].shape[1]
    show = [[row[:, wide - 2 : wide - 1] for row in level] for level in rows]
    fold = [[row[:, wide - 1 : wide] for row in level] for level in rows]
    return show, fold


def wide_row(store, place, row_ref):
    hands = row_ref.shape[1]
    store[place : place + 1, 0:hands] = row_ref[...]
    return store[place : place + 1, :]


def first_kernel(
    node_count,
    parent_ref,
    home_ref,
    from_left_ref,
    from_right_ref,
    from_far_ref,
    one_ref,
    two_ref,
    block_ref,
    chain_ref,
    value_ref,
    square_ref,
    window,
    ranges,
    cols,
    pay,
):
    _, tiles, slots, _ = home_ref.shape
    off_one, off_two, off_three = level_offsets(parent_ref, node_count, slots)
    window[0, :, 0:slots] = from_left_ref[...]
    window[0, :, slots : 2 * slots] = home_ref[0]
    window[1, :, 0:slots] = home_ref[1]
    window[2, :, 0:slots] = home_ref[2]
    window[2, :, slots : 2 * slots] = from_right_ref[0]
    window[3, :, 0:slots] = home_ref[3]
    window[3, :, slots : 2 * slots] = from_right_ref[1]
    window[3, :, 2 * slots : 3 * slots - 8] = from_far_ref[...]
    starts = [slots - 4 * off_one, 0, 4 * off_two, 4 * (off_two + off_three)]
    point = []
    for idx in range(4):
        rows = []
        for slot in range(4):
            place = pl.ds(starts[idx] + slot, slots // 4, stride=4)
            row = jnp.concatenate([window[idx, tile, place, :] for tile in range(tiles)], axis=1)
            chain_ref[idx, slot] = row
            rows.append(row)
        point.append(rows)
    show, fold = scale_columns(point)
    ranges[...] = jnp.zeros(ranges.shape, jnp.float32)
    range_one = wide_row(ranges, 0, one_ref)
    range_two = wide_row(ranges, 1, two_ref)
    found = operator_q(point, show, fold, range_one, range_two, block_ref, cols, pay)
    for idx in range(4):
        for slot in range(4):
            value_ref[idx, slot] = found[idx][slot]
    square_ref[...] = squares(found)


def rate_of(parts_ref, entry_count):
    square_sum = jnp.sum(parts_ref[...], axis=0, keepdims=True)[:, 0:1]
    return step_scale / jnp.sqrt(square_sum / entry_count + eps_value)


def second_kernel(
    entry_count,
    chain_ref,
    value_ref,
    parts_ref,
    one_ref,
    two_ref,
    block_ref,
    own_ref,
    left_ref,
    right_ref,
    far_ref,
    square_ref,
    ranges,
    cols,
    pay,
):
    _, tiles, slots, _ = own_ref.shape
    rate = rate_of(parts_ref, entry_count)
    raw = [[chain_ref[idx, slot] for slot in range(4)] for idx in range(4)]
    show, fold = scale_columns(raw)
    point = [
        [raw[idx][slot] + rate * value_ref[idx, slot] for slot in range(4)] for idx in range(4)
    ]
    ranges[...] = jnp.zeros(ranges.shape, jnp.float32)
    range_one = wide_row(ranges, 0, one_ref)
    range_two = wide_row(ranges, 1, two_ref)
    found = operator_q(point, show, fold, range_one, range_two, block_ref, cols, pay)
    square_ref[...] = squares(found)
    for idx in range(4):
        for slot in range(4):
            for tile in range(tiles):
                part = found[idx][slot][:, tile * LANES : (tile + 1) * LANES]
                own_ref[idx, tile, pl.ds(slot, slots // 4, stride=4), :] = part
    left_ref[...] = own_ref[0]
    right_ref[...] = own_ref[2:4]
    far_ref[...] = own_ref[3, :, 8:slots, :]


def last_kernel(
    node_count,
    entry_count,
    hands,
    parent_ref,
    own_ref,
    from_right_ref,
    from_left_ref,
    from_far_ref,
    parts_ref,
    logits_ref,
    new_ref,
    half_ref,
    window,
):
    _, tiles, slots, _ = own_ref.shape
    off_one, off_two, off_three = level_offsets(parent_ref, node_count, slots)
    rate = rate_of(parts_ref, entry_count)
    window[0, :, 0:slots] = own_ref[0]
    window[0, :, slots : 2 * slots] = from_right_ref[...]
    window[1, :, 0:slots] = own_ref[1]
    window[2, :, 0:slots] = from_left_ref[0]
    window[2, :, slots : 2 * slots] = own_ref[2]
    window[3, :, 8:slots] = from_far_ref[...]
    window[3, :, slots : 2 * slots] = from_left_ref[1]
    window[3, :, 2 * slots : 3 * slots] = own_ref[3]
    starts = [4 * off_one, 0, slots - 4 * off_two, 2 * slots - 4 * (off_two + off_three)]
    for idx in range(4):
        for tile in range(tiles):
            start = tile * LANES
            stop = min(start + LANES, hands)
            value = window[idx, tile, pl.ds(starts[idx], slots), :][:, 0 : stop - start]
            half_ref[0, idx, :, start:stop] = value
            new_ref[0, idx, :, start:stop] = logits_ref[0, idx, :, start:stop] + rate * value


def shared_parts(part):
    count = lax.axis_size("node") * lax.axis_size("board")
    spread = jnp.broadcast_to(part, (count, LANES))
    return lax.all_to_all(spread, ("node", "board"), 0, 0, tiled=True)


def per_device(
    logits, pot_size, node_type, parent_slot, range_one, range_two, hand_rank, live_mask
):
    _, levels, slots, hands = logits.shape
    wide = padded(hands)
    groups = slots // 4
    node_count = lax.axis_size("node")
    entry_count = float(logits.size * node_count * lax.axis_size("board"))
    vmem = pl.BlockSpec(memory_space=pltpu.VMEM)
    smem = pl.BlockSpec(memory_space=pltpu.SMEM)
    f32 = jnp.float32
    home, to_right, to_left, to_far = packed_rows(logits, pot_size, node_type)
    from_left = passed_along(to_right, "node", 1)
    from_right = passed_along(to_left, "node", -1)
    from_far = passed_along(to_far, "node", -2)
    blocks = payoff_blocks(hand_rank, live_mask)
    rows = 7 * slots
    work = [
        pltpu.VMEM((8, wide), f32),
        pltpu.VMEM((rows, 2 * wide), jnp.bfloat16),
        pltpu.VMEM((rows, wide), f32),
    ]
    chain_shape = jax.ShapeDtypeStruct((levels, 4, groups, wide), f32)
    square_shape = jax.ShapeDtypeStruct((1, LANES), f32)
    limit = pltpu.CompilerParams(vmem_limit_bytes=32 * MEBI)
    cost = pl.CostEstimate(
        flops=4 * rows * wide * wide, bytes_accessed=6 * wide * wide, transcendentals=0
    )
    chain, value, part = pl.pallas_call(
        functools.partial(first_kernel, node_count),
        out_shape=(chain_shape, chain_shape, square_shape),
        in_specs=[smem] + [vmem] * 7,
        scratch_shapes=[pltpu.VMEM((levels, wide // LANES, 3 * slots, LANES), f32)] + work,
        compiler_params=limit,
        cost_estimate=cost,
        name="first",
    )(parent_slot, home, from_left, from_right, from_far, range_one, range_two, blocks)
    parts = shared_parts(part)
    own, to_left, to_right, to_far, part = pl.pallas_call(
        functools.partial(second_kernel, entry_count),
        out_shape=message_shapes(levels, slots, wide) + (square_shape,),
        in_specs=[vmem] * 6,
        scratch_shapes=work,
        compiler_params=limit,
        cost_estimate=cost,
        name="second",
    )(chain, value, parts, range_one, range_two, blocks)
    from_right = passed_along(to_left, "node", -1)
    from_left = passed_along(to_right, "node", 1)
    from_far = passed_along(to_far, "node", 2)
    parts = shared_parts(part)
    out_shape = jax.ShapeDtypeStruct(logits.shape, f32)
    return pl.pallas_call(
        functools.partial(last_kernel, node_count, entry_count, hands),
        out_shape=(out_shape, out_shape),
        in_specs=[smem] + [vmem] * 6,
        scratch_shapes=[pltpu.VMEM((levels, wide // LANES, 3 * slots, LANES), f32)],
        compiler_params=pltpu.CompilerParams(vmem_limit_bytes=20 * MEBI),
        name="last",
    )(parent_slot, own, from_right, from_left, from_far, parts, logits)


def solution(mesh):
    return jax.shard_map(
        per_device,
        mesh=mesh,
        in_specs=(
            P("board", None, "node", None),
            P(None, "node"),
            P(None, "node"),
            P(None, "node"),
            P("board", None),
            P("board", None),
            P("board", None),
            P("board", None),
        ),
        out_specs=(P("board", None, "node", None), P("board", None, "node", None)),
        check_vma=False,
    )
```

time: 263 us -> 60.7 us (0.23)
  waiting for transfers between devices: 76.3 us -> 5.67 us
  blocking collectives: 81.1 us -> 25.1 us
  matrix products: 30.1 us -> 0 us
  local copies, waits for them, and re-layouts: 28.7 us -> 4.59 us
  other arithmetic: 19.7 us -> 0 us
  Pallas kernels: 0 us -> 10.5 us
  starting transfers between devices: 22.2 us -> 13.8 us
  between operations: 3.67 us -> 0.73 us
    psum x2 -> x0, blocking collectives: 81.1 us -> none  [rate_for(): lax.psum(jnp.sum(values_found * values_found), ('node', 'board'))]
    ppermute x21 -> x6, waiting for transfers between devices: 76.3 us -> 5.67 us  [passed_along(): return lax.ppermute(value, axis, pairs)]
    dot_general x34 -> x0, matrix products: 30.1 us -> none  [the longest x2 7.3 us: terminal_pay(): jnp.einsum('bij,bnj->bni', show_block, show_cols, preferred_element_type=...]
    all_to_all x0 -> x2, blocking collectives: none -> 25.1 us  [shared_parts(): return lax.all_to_all(spread, ('node', 'board'), 0, 0, tiled=True)]
    gather x22 -> x0, local copies, waits for them, and re-layouts: 14.6 us -> none  [the longest x6 4.17 us: reach_levels(): above_one = jnp.take(window_one, local_idx, axis=1)]
    pallas_call x0 -> x5, Pallas kernels: none -> 10.5 us  [the longest x1 3.37 us: per_device(): pl.pallas_call(functools.partial(first_kernel, node_count), out_shape=(ch...]
    ppermute x21 -> x6, starting transfers between devices: 22.2 us -> 13.8 us  [passed_along(): return lax.ppermute(value, axis, pairs)]
    slice x9 -> x0, local copies, waits for them, and re-layouts: 4.95 us -> none  [the longest x4 2.64 us: terminal_pay(): pay_one = product[:, :column_count].reshape(boards, LEVELS, SLOT_DEV, HANDS)]
  transfers between devices with their start and end apart: 21 -> 6, of which waited for: 14 -> 1; matrix products, arithmetic and copies ran while one was open for 11% -> 0% of each run, Pallas kernels for 0% -> 4%
where the time goes in v1:
time: 60.7 us; the launch traced here: 60.3 us
  blocking collectives  25.1 us (41%)
  starting transfers between devices  13.8 us (23%)
  Pallas kernels  10.5 us (17%)
  waiting for transfers between devices  5.67 us (9%)
  local copies, waits for them, and re-layouts  4.59 us (8%)
  between operations  0.73 us (1%)
    all_to_all x2, blocking collectives, shared_parts(): return lax.all_to_all(spread, ('node', 'board'), 0, 0, tiled=True)  25.1 us
    ppermute x6, starting transfers between devices, passed_along(): return lax.ppermute(value, axis, pairs)  13.8 us
    ppermute x6, waiting for transfers between devices, passed_along(): return lax.ppermute(value, axis, pairs)  5.67 us
    unnamed x20, local copies, waits for them, and re-layouts  4.57 us
    pallas_call x1, Pallas kernels, per_device(): pl.pallas_call(functools.partial(first_kernel, node_count), out_shape=(ch...  3.37 us
    pallas_call x1, Pallas kernels, per_device(): pl.pallas_call(functools.partial(second_kernel, entry_count), out_shape=m...  2.86 us
    pallas_call x1, Pallas kernels, payoff_blocks(): pl.pallas_call(functools.partial(payoff_kernel, hands), out_shape=jax.Sha...  2.14 us
    pallas_call x1, Pallas kernels, per_device(): pl.pallas_call(functools.partial(last_kernel, node_count, entry_count, ha...  1.86 us
  transfers between devices with their start and end apart: 6, of which 1 were waited for; matrix products, arithmetic and copies ran while one was open for 0% of the time, Pallas kernels for 4%

profile of v1, /device:TPU:0, one launch (start us, length us, event | category | flops | bytes accessed | tf_op | source)
XLA Modules:
  0.0 60.3 jit_solution(12887394892865393217)
XLA Ops:
  0.6 0.0 copy-start
  0.6 1.1 %copy-done = f32[1,4,32,1326]{3,2,1,0:T(8,128)S(1)} copy-done((f32[1,4,32,1326]{3,2,1,0:T(8,128)S(1)}, f32[1,4,32,1326]{3,2,1,0:T(8,128)}, u32[]{:S(2)}) %copy-start) | copy-done | bytes 678936
  1.7 0.0 copy-start.8
  1.7 0.7 %copy-done.8 = f32[4,32]{1,0:T(4,128)S(1)} copy-done((f32[4,32]{1,0:T(4,128)S(1)}, f32[4,32]{1,0:T(4,128)}, u32[]{:S(2)}) %copy-start.8) | copy-done | bytes 536
  2.4 0.0 copy-start.9
  2.4 0.7 %copy-done.9 = s32[4,32]{1,0:T(4,128)S(1)} copy-done((s32[4,32]{1,0:T(4,128)S(1)}, s32[4,32]{1,0:T(4,128)}, u32[]{:S(2)}) %copy-start.9) | copy-done | bytes 536
  3.1 0.0 copy-start.2
  3.1 0.0 copy-start.3
  3.1 0.0 copy-start.5
  3.1 0.2 pack.1
  3.3 7.0 %collective-permute-start.1 = (f32[2,11,32,128]{3,2,1,0:T(8,128)S(1)}, f32[2,11,32,128]{3,2,1,0:T(8,128)S(1)}, u32[]{:S(2)}, u32[]{:S(2)}) collective-permute-start(f32[2,11,32,128]{3,2,1,0:T(8,128)S(1)} %get-tuple-element.16), channel_id=1, source_target_pairs={{0,30},{2,0},{4,2},{6,4},{8,6},{10,8},{12,10},{14,12},{16,14},{18,... | collective-permute-start | bytes 1081352 | tf_op jit(solution)/shard_map/ppermute | solution.py:25
  10.3 0.0 collective-permute-start
  10.3 1.1 %collective-permute-start.2 = (f32[11,24,128]{2,1,0:T(8,128)S(1)}, f32[11,24,128]{2,1,0:T(8,128)S(1)}, u32[]{:S(2)}, u32[]{:S(2)}) collective-permute-start(f32[11,24,128]{2,1,0:T(8,128)S(1)} %get-tuple-element.17), channel_id=1, source_target_pairs={{0,28},{2,30},{4,0},{6,2},{8,4},{10,6},{12,8},{14,10},{16,12},{18,... | collective-permute-start | bytes 405512 | tf_op jit(solution)/shard_map/ppermute | solution.py:25
  11.4 0.0 copy-start.4
  11.4 0.7 %copy-done.4 = s32[2,1408]{1,0:T(2,128)S(1)} copy-done((s32[2,1408]{1,0:T(2,128)S(1)}, s32[2,1408]{1,0:T(2,128)}, u32[]{:S(2)}) %copy-start.4) | copy-done | bytes 11288
  12.1 0.0 copy-start.6
  12.1 0.7 %copy-done.6 = s32[1,1326]{1,0:T(1,128)S(1)} copy-done((s32[1,1326]{1,0:T(1,128)S(1)}, s32[1,1326]{1,0:T(1,128)}, u32[]{:S(2)}) %copy-start.6) | copy-done | bytes 5328
  12.8 0.0 copy-start.7
  12.8 0.7 %copy-done.7 = s32[1,1326]{1,0:T(1,128)S(1)} copy-done((s32[1,1326]{1,0:T(1,128)S(1)}, s32[1,1326]{1,0:T(1,128)}, u32[]{:S(2)}) %copy-start.7) | copy-done | bytes 5328
  13.5 2.1 %payoff.1.block_ref = bf16[2816,1408]{1,0:T(8,128)(2,1)S(1)} custom-call(s32[2,1408]{1,0:T(2,128)S(1)} %copy-done.4, s32[1,1326]{1,0:T(1,128)S(1)} %copy-done.6, s32[1,1326]{1,0:T(1,128)S(1)} %copy-done.7), custom_call_target="tpu_custom_call" | custom-call | flops 507510784 | bytes 7929856 | tf_op jit(solution)/shard_map/payoff/pallas_call | solution.py:63
  15.7 5.7 %collective-permute-done.2.from_far_ref = f32[11,24,128]{2,1,0:T(8,128)S(1)} collective-permute-done((f32[11,24,128]{2,1,0:T(8,128)S(1)}, f32[11,24,128]{2,1,0:T(8,128)S(1)}, u32[]{:S(2)}, u32[]{:S(2)}) %collective-permute-start.2) | collective-permute-done | bytes 135200 | tf_op jit(solution)/shard_map/ppermute | solution.py:25
  21.3 0.0 collective-permute-done.from_left_ref
  21.3 0.0 collective-permute-done.1.from_right_ref
  21.3 0.0 copy-done.2
  21.3 0.0 copy-done.3
  21.4 0.0 copy-done.5
  21.4 0.0 copy-start.1
  21.4 3.4 %first.1 = (f32[4,4,8,1408]{3,2,1,0:T(8,128)S(1)}, f32[4,4,8,1408]{3,2,1,0:T(8,128)S(1)}, f32[1,128]{1,0:T(1,128)S(1)}) custom-call(s32[4,32]{1,0:T(4,128)S(1)} %copy-done.5, f32[4,11,32,128]{3,2,1,0:T(8,128)S(1)} %get-tuple-element.14.home_ref, f32[11,32,128]{2,1,0:T(8,128)S(1)} %collective-permute-done.from_left_ref, ...), custom_call_target="tpu_custom_call" | custom-call | flops 1776287744 | bytes 11894784 | tf_op jit(solution)/shard_map/first/pallas_call | solution.py:392
  24.8 13.0 %all_to_all.16 = f32[32,1,128]{2,1,0:T(1,128)S(1)} all-to-all(f32[32,1,128]{2,1,0:T(1,128)S(1)} %broadcast_in_dim.4), channel_id=1, replica_groups=mesh['node'=16,'board'=2] {'node','board'}, dimensions={0} | all-to-all | bytes 32768 | tf_op jit(solution)/shard_map/all_to_all | solution.py:361
  37.8 2.9 %second.1 = (f32[4,11,32,128]{3,2,1,0:T(8,128)S(1)}, f32[11,32,128]{2,1,0:T(8,128)S(1)}, f32[2,11,32,128]{3,2,1,0:T(8,128)S(1)}, f32[11,24,128]{2,1,0:T(8,128)S(1)}, f32[1,128]{1,0:T(1,128)S(1)}) custom-call(f32[4,4,8,1408]{3,2,1,0:T(8,128)S(1)} %get-tuple-element.18.chain_ref, f32[4,4,8,1408]{3,2,1,0:T(8,128)S(1)} %get-tuple-element.19.value_ref, ...), custom_call_target="tpu_custom_call" | custom-call | flops 1776287744 | bytes 11894784 | tf_op jit(solution)/shard_map/second/pallas_call | solution.py:402
  40.7 0.6 collective-permute-start.4
  41.3 5.1 %collective-permute-start.3 = (f32[11,32,128]{2,1,0:T(8,128)S(1)}, f32[11,32,128]{2,1,0:T(8,128)S(1)}, u32[]{:S(2)}, u32[]{:S(2)}) collective-permute-start(f32[11,32,128]{2,1,0:T(8,128)S(1)} %get-tuple-element.22), channel_id=1, source_target_pairs={{0,30},{2,0},{4,2},{6,4},{8,6},{10,8},{12,10},{14,12},{16,14},{18,... | collective-permute-start | bytes 540680 | tf_op jit(solution)/shard_map/ppermute | solution.py:25
  46.4 0.0 collective-permute-start.5
  46.4 12.0 %all_to_all.17 = f32[32,1,128]{2,1,0:T(1,128)S(1)} all-to-all(f32[32,1,128]{2,1,0:T(1,128)S(1)} %broadcast_in_dim.5), channel_id=1, replica_groups=mesh['node'=16,'board'=2] {'node','board'}, dimensions={0} | all-to-all | bytes 32768 | tf_op jit(solution)/shard_map/all_to_all | solution.py:361
  58.4 0.0 collective-permute-done.5.from_far_ref
  58.4 0.0 collective-permute-done.3.from_right_ref
  58.4 0.0 collective-permute-done.4.from_left_ref
  58.4 0.0 copy-done.1
  58.4 1.9 %last.1 = (f32[1,4,32,1326]{3,2,1,0:T(8,128)}, f32[1,4,32,1326]{3,2,1,0:T(8,128)}) custom-call(s32[4,32]{1,0:T(4,128)S(1)} %copy-done.5, f32[4,11,32,128]{3,2,1,0:T(8,128)S(1)} %get-tuple-element.21.own_ref, f32[11,32,128]{2,1,0:T(8,128)S(1)} %collective-permute-done.3.from_right_ref, f32[2,11,32,128]{3,2,1,0:T(8,128)S(1)} %collective-permute-done.4.from_left_ref, ...), custom_call_target="tpu_custom_call" | custom-call | tf_op jit(solution)/shard_map/last/pallas_call | solution.py:416
  (2 shorter events, 0.0 us)
Async XLA Ops:
  0.6 1.1 %copy-start = (f32[1,4,32,1326]{3,2,1,0:T(8,128)S(1)}, f32[1,4,32,1326]{3,2,1,0:T(8,128)}, u32[]{:S(2)}) copy-start(f32[1,4,32,1326]{3,2,1,0:T(8,128)} %logits_ref.3) | copy-start | bytes 2036740
  1.7 0.7 %copy-start.8 = (f32[4,32]{1,0:T(4,128)S(1)}, f32[4,32]{1,0:T(4,128)}, u32[]{:S(2)}) copy-start(f32[4,32]{1,0:T(4,128)} %pot_ref.1) | copy-start | bytes 1540
  2.4 0.7 %copy-start.9 = (s32[4,32]{1,0:T(4,128)S(1)}, s32[4,32]{1,0:T(4,128)}, u32[]{:S(2)}) copy-start(s32[4,32]{1,0:T(4,128)} %kind_ref.1) | copy-start | bytes 1540
  3.1 18.2 %copy-start.2 = (f32[1,1326]{1,0:T(1,128)S(1)}, f32[1,1326]{1,0:T(1,128)}, u32[]{:S(2)}) copy-start(f32[1,1326]{1,0:T(1,128)} %one_ref.3) | copy-start | bytes 15916
  3.1 18.2 %copy-start.3 = (f32[1,1326]{1,0:T(1,128)S(1)}, f32[1,1326]{1,0:T(1,128)}, u32[]{:S(2)}) copy-start(f32[1,1326]{1,0:T(1,128)} %two_ref.3) | copy-start | bytes 15916
  3.1 18.2 %copy-start.5 = (s32[4,32]{1,0:T(4,128)S(1)}, s32[4,32]{1,0:T(4,128)}, u32[]{:S(2)}) copy-start(s32[4,32]{1,0:T(4,128)} %parent_ref.3) | copy-start | bytes 1540
  3.3 18.0 %collective-permute-start.1 = (f32[2,11,32,128]{3,2,1,0:T(8,128)S(1)}, f32[2,11,32,128]{3,2,1,0:T(8,128)S(1)}, u32[]{:S(2)}, u32[]{:S(2)}) collective-permute-start(f32[2,11,32,128]{3,2,1,0:T(8,128)S(1)} %get-tuple-element.16), channel_id=1, source_target_pairs={{0,30},{2,0},{4,2},{6,4},{8,6},{10,8},{12,10},{14,12},{16,14},{18,... | collective-permute-start | bytes 1081352 | tf_op jit(solution)/shard_map/ppermute | solution.py:25
  10.3 11.0 %collective-permute-start = (f32[11,32,128]{2,1,0:T(8,128)S(1)}, f32[11,32,128]{2,1,0:T(8,128)S(1)}, u32[]{:S(2)}, u32[]{:S(2)}) collective-permute-start(f32[11,32,128]{2,1,0:T(8,128)S(1)} %get-tuple-element.15), channel_id=1, source_target_pairs={{0,2},{2,4},{4,6},{6,8},{8,10},{10,12},{12,14},{14,16},{16,18},{18... | collective-permute-start | bytes 540680 | tf_op jit(solution)/shard_map/ppermute | solution.py:25
  10.3 11.0 %collective-permute-start.2 = (f32[11,24,128]{2,1,0:T(8,128)S(1)}, f32[11,24,128]{2,1,0:T(8,128)S(1)}, u32[]{:S(2)}, u32[]{:S(2)}) collective-permute-start(f32[11,24,128]{2,1,0:T(8,128)S(1)} %get-tuple-element.17), channel_id=1, source_target_pairs={{0,28},{2,30},{4,0},{6,2},{8,4},{10,6},{12,8},{14,10},{16,12},{18,... | collective-permute-start | bytes 405512 | tf_op jit(solution)/shard_map/ppermute | solution.py:25
  11.4 0.7 %copy-start.4 = (s32[2,1408]{1,0:T(2,128)S(1)}, s32[2,1408]{1,0:T(2,128)}, u32[]{:S(2)}) copy-start(s32[2,1408]{1,0:T(2,128)} %constant.2.clone.cards_ref) | copy-start | bytes 33796
  12.1 0.7 %copy-start.6 = (s32[1,1326]{1,0:T(1,128)S(1)}, s32[1,1326]{1,0:T(1,128)}, u32[]{:S(2)}) copy-start(s32[1,1326]{1,0:T(1,128)} %rank_ref.1) | copy-start | bytes 15916
  12.8 0.7 %copy-start.7 = (s32[1,1326]{1,0:T(1,128)S(1)}, s32[1,1326]{1,0:T(1,128)}, u32[]{:S(2)}) copy-start(s32[1,1326]{1,0:T(1,128)} %live_ref.1) | copy-start | bytes 15916
  21.4 37.1 %copy-start.1 = (f32[1,4,32,1326]{3,2,1,0:T(8,128)S(1)}, f32[1,4,32,1326]{3,2,1,0:T(8,128)}, u32[]{:S(2)}) copy-start(f32[1,4,32,1326]{3,2,1,0:T(8,128)} %logits_ref.3) | copy-start | bytes 2036740
  40.7 17.7 %collective-permute-start.4 = (f32[2,11,32,128]{3,2,1,0:T(8,128)S(1)}, f32[2,11,32,128]{3,2,1,0:T(8,128)S(1)}, u32[]{:S(2)}, u32[]{:S(2)}) collective-permute-start(f32[2,11,32,128]{3,2,1,0:T(8,128)S(1)} %get-tuple-element.23), channel_id=1, source_target_pairs={{0,2},{2,4},{4,6},{6,8},{8,10},{10,12},{12,14},{14,16},{16,18},{18... | collective-permute-start | bytes 1081352 | tf_op jit(solution)/shard_map/ppermute | solution.py:25
  41.3 17.2 %collective-permute-start.3 = (f32[11,32,128]{2,1,0:T(8,128)S(1)}, f32[11,32,128]{2,1,0:T(8,128)S(1)}, u32[]{:S(2)}, u32[]{:S(2)}) collective-permute-start(f32[11,32,128]{2,1,0:T(8,128)S(1)} %get-tuple-element.22), channel_id=1, source_target_pairs={{0,30},{2,0},{4,2},{6,4},{8,6},{10,8},{12,10},{14,12},{16,14},{18,... | collective-permute-start | bytes 540680 | tf_op jit(solution)/shard_map/ppermute | solution.py:25
  46.4 12.1 %collective-permute-start.5 = (f32[11,24,128]{2,1,0:T(8,128)S(1)}, f32[11,24,128]{2,1,0:T(8,128)S(1)}, u32[]{:S(2)}, u32[]{:S(2)}) collective-permute-start(f32[11,24,128]{2,1,0:T(8,128)S(1)} %get-tuple-element.24), channel_id=1, source_target_pairs={{0,4},{2,6},{4,8},{6,10},{8,12},{10,14},{12,16},{14,18},{16,20},{1... | collective-permute-start | bytes 405512 | tf_op jit(solution)/shard_map/ppermute | solution.py:25

commit v2 on v1

--- a/solution.py
+++ b/solution.py
@@ -355,10 +355,27 @@
             new_ref[0, idx, :, start:stop] = logits_ref[0, idx, :, start:stop] + rate * value
 
 
-def shared_parts(part):
-    count = lax.axis_size("node") * lax.axis_size("board")
+def swapped_sum(part, axis, groups=None):
+    count = len(groups[0]) if groups else lax.axis_size(axis)
     spread = jnp.broadcast_to(part, (count, LANES))
-    return lax.all_to_all(spread, ("node", "board"), 0, 0, tiled=True)
+    got = lax.all_to_all(spread, axis, 0, 0, axis_index_groups=groups, tiled=True)
+    return jnp.sum(got, axis=0, keepdims=True)
+
+
+def staged_parts(part):
+    count = lax.axis_size("node")
+    inner = 1
+    while inner * inner < count:
+        inner *= 2
+    near = [list(range(start, start + inner)) for start in range(0, count, inner)]
+    across = [list(range(start, count, inner)) for start in range(inner)]
+    part = swapped_sum(part, "board")
+    part = swapped_sum(part, "node", near)
+    return swapped_sum(part, "node", across)
+
+
+def gathered_parts(part):
+    return lax.all_gather(part, ("node", "board"), axis=0, tiled=True)
 
 
 def per_device(
@@ -398,7 +415,7 @@
         cost_estimate=cost,
         name="first",
     )(parent_slot, home, from_left, from_right, from_far, range_one, range_two, blocks)
-    parts = shared_parts(part)
+    parts = gathered_parts(part)
     own, to_left, to_right, to_far, part = pl.pallas_call(
         functools.partial(second_kernel, entry_count),
         out_shape=message_shapes(levels, slots, wide) + (square_shape,),
@@ -411,7 +428,7 @@
     from_right = passed_along(to_left, "node", -1)
     from_left = passed_along(to_right, "node", 1)
     from_far = passed_along(to_far, "node", 2)
-    parts = shared_parts(part)
+    parts = staged_parts(part)
     out_shape = jax.ShapeDtypeStruct(logits.shape, f32)
     return pl.pallas_call(
         functools.partial(last_kernel, node_count, entry_count, hands),

time: 60.7 us -> 98.8 us (1.63)
  blocking collectives: 25.1 us -> 63.1 us
    all_gather x0 -> x1, blocking collectives: none -> 41.8 us  [gathered_parts(): return lax.all_gather(part, ('node', 'board'), axis=0, tiled=True)]
    all_to_all x2 -> x3, blocking collectives: 25.1 us -> 21.3 us  [swapped_sum(): lax.all_to_all(spread, axis, 0, 0, axis_index_groups=groups, tiled=True)]
  transfers between devices with their start and end apart: 6 -> 6, of which waited for: 1 -> 1; matrix products, arithmetic and copies ran while one was open for 0% -> 0% of each run, Pallas kernels for 4% -> 2%
where the time goes in v2:
time: 98.8 us; the launch traced here: 98.3 us
  blocking collectives  63.1 us (64%)
  starting transfers between devices  13.8 us (14%)
  Pallas kernels  10.4 us (11%)
  waiting for transfers between devices  5.67 us (6%)
  local copies, waits for them, and re-layouts  4.58 us (5%)
    all_gather x1, blocking collectives, gathered_parts(): return lax.all_gather(part, ('node', 'board'), axis=0, tiled=True)  41.8 us
    all_to_all x3, blocking collectives, swapped_sum(): lax.all_to_all(spread, axis, 0, 0, axis_index_groups=groups, tiled=True)  21.3 us
    ppermute x6, starting transfers between devices, passed_along(): return lax.ppermute(value, axis, pairs)  13.8 us
    ppermute x6, waiting for transfers between devices, passed_along(): return lax.ppermute(value, axis, pairs)  5.67 us
    unnamed x20, local copies, waits for them, and re-layouts  4.57 us
    pallas_call x1, Pallas kernels, per_device(): pl.pallas_call(functools.partial(first_kernel, node_count), out_shape=(ch...  3.37 us
    pallas_call x1, Pallas kernels, per_device(): pl.pallas_call(functools.partial(second_kernel, entry_count), out_shape=m...  2.85 us
    pallas_call x1, Pallas kernels, payoff_blocks(): pl.pallas_call(functools.partial(payoff_kernel, hands), out_shape=jax.Sha...  2.14 us
  transfers between devices with their start and end apart: 6, of which 1 were waited for; matrix products, arithmetic and copies ran while one was open for 0% of the time, Pallas kernels for 2%

profile of v2, /device:TPU:0, one launch (start us, length us, event | category | flops | bytes accessed | tf_op | source)
XLA Modules:
  0.0 98.3 jit_solution(1224802029621514742)
XLA Ops:
  0.6 0.0 copy-start
  0.6 1.1 %copy-done = f32[1,4,32,1326]{3,2,1,0:T(8,128)S(1)} copy-done((f32[1,4,32,1326]{3,2,1,0:T(8,128)S(1)}, f32[1,4,32,1326]{3,2,1,0:T(8,128)}, u32[]{:S(2)}) %copy-start) | copy-done | bytes 678936
  1.7 0.0 copy-start.8
  1.7 0.7 copy-done.8
  2.4 0.0 copy-start.9
  2.4 0.7 copy-done.9
  3.1 0.0 copy-start.2
  3.1 0.0 copy-start.3
  3.1 0.0 copy-start.5
  3.1 0.2 pack.1
  3.3 7.0 %collective-permute-start.1 = (f32[2,11,32,128]{3,2,1,0:T(8,128)S(1)}, f32[2,11,32,128]{3,2,1,0:T(8,128)S(1)}, u32[]{:S(2)}, u32[]{:S(2)}) collective-permute-start(f32[2,11,32,128]{3,2,1,0:T(8,128)S(1)} %get-tuple-element.16), channel_id=1, source_target_pairs={{0,30},{2,0},{4,2},{6,4},{8,6},{10,8},{12,10},{14,12},{16,14},{18,... | collective-permute-start | bytes 1081352 | tf_op jit(solution)/shard_map/ppermute | solution.py:25
  10.3 0.0 collective-permute-start
  10.3 1.1 %collective-permute-start.2 = (f32[11,24,128]{2,1,0:T(8,128)S(1)}, f32[11,24,128]{2,1,0:T(8,128)S(1)}, u32[]{:S(2)}, u32[]{:S(2)}) collective-permute-start(f32[11,24,128]{2,1,0:T(8,128)S(1)} %get-tuple-element.17), channel_id=1, source_target_pairs={{0,28},{2,30},{4,0},{6,2},{8,4},{10,6},{12,8},{14,10},{16,12},{18,... | collective-permute-start | bytes 405512 | tf_op jit(solution)/shard_map/ppermute | solution.py:25
  11.4 0.0 copy-start.4
  11.4 0.7 copy-done.4
  12.1 0.0 copy-start.6
  12.1 0.7 copy-done.6
  12.8 0.0 copy-start.7
  12.8 0.7 copy-done.7
  13.5 2.1 %payoff.1.block_ref = bf16[2816,1408]{1,0:T(8,128)(2,1)S(1)} custom-call(s32[2,1408]{1,0:T(2,128)S(1)} %copy-done.4, s32[1,1326]{1,0:T(1,128)S(1)} %copy-done.6, s32[1,1326]{1,0:T(1,128)S(1)} %copy-done.7), custom_call_target="tpu_custom_call" | custom-call | flops 507510784 | bytes 7929856 | tf_op jit(solution)/shard_map/payoff/pallas_call | solution.py:63
  15.7 5.7 %collective-permute-done.2.from_far_ref = f32[11,24,128]{2,1,0:T(8,128)S(1)} collective-permute-done((f32[11,24,128]{2,1,0:T(8,128)S(1)}, f32[11,24,128]{2,1,0:T(8,128)S(1)}, u32[]{:S(2)}, u32[]{:S(2)}) %collective-permute-start.2) | collective-permute-done | bytes 135200 | tf_op jit(solution)/shard_map/ppermute | solution.py:25
  21.3 0.0 collective-permute-done.from_left_ref
  21.3 0.0 collective-permute-done.1.from_right_ref
  21.3 0.0 copy-done.2
  21.3 0.0 copy-done.3
  21.4 0.0 copy-done.5
  21.4 0.0 copy-start.1
  21.4 3.4 %first.1 = (f32[4,4,8,1408]{3,2,1,0:T(8,128)S(1)}, f32[4,4,8,1408]{3,2,1,0:T(8,128)S(1)}, f32[1,128]{1,0:T(1,128)S(1)}) custom-call(s32[4,32]{1,0:T(4,128)S(1)} %copy-done.5, f32[4,11,32,128]{3,2,1,0:T(8,128)S(1)} %get-tuple-element.14.home_ref, f32[11,32,128]{2,1,0:T(8,128)S(1)} %collective-permute-done.from_left_ref, ...), custom_call_target="tpu_custom_call" | custom-call | flops 1776287744 | bytes 11894784 | tf_op jit(solution)/shard_map/first/pallas_call | solution.py:409
  24.8 41.8 %all-gather = f32[32,1,128]{2,1,0:T(1,128)S(1)} all-gather(f32[1,1,128]{2,1,0:T(1,128)S(1)} %bitcast.9), channel_id=1, replica_groups=mesh['node'=16,'board'=2] {'node','board'}, dimensions={0}, use_global_device_ids=true | all-gather | bytes 16896 | tf_op jit(solution)/shard_map/all_gather | solution.py:378
  66.6 2.8 %second.1 = (f32[4,11,32,128]{3,2,1,0:T(8,128)S(1)}, f32[11,32,128]{2,1,0:T(8,128)S(1)}, f32[2,11,32,128]{3,2,1,0:T(8,128)S(1)}, f32[11,24,128]{2,1,0:T(8,128)S(1)}, f32[1,128]{1,0:T(1,128)S(1)}) custom-call(f32[4,4,8,1408]{3,2,1,0:T(8,128)S(1)} %get-tuple-element.18.chain_ref, f32[4,4,8,1408]{3,2,1,0:T(8,128)S(1)} %get-tuple-element.19.value_ref, ...), custom_call_target="tpu_custom_call" | custom-call | flops 1776287744 | bytes 11894784 | tf_op jit(solution)/shard_map/second/pallas_call | solution.py:419
  69.4 0.1 collective-permute-start.4
  69.5 5.6 %collective-permute-start.3 = (f32[11,32,128]{2,1,0:T(8,128)S(1)}, f32[11,32,128]{2,1,0:T(8,128)S(1)}, u32[]{:S(2)}, u32[]{:S(2)}) collective-permute-start(f32[11,32,128]{2,1,0:T(8,128)S(1)} %get-tuple-element.22), channel_id=1, source_target_pairs={{0,30},{2,0},{4,2},{6,4},{8,6},{10,8},{12,10},{14,12},{16,14},{18,... | collective-permute-start | bytes 540680 | tf_op jit(solution)/shard_map/ppermute | solution.py:25
  75.1 0.0 collective-permute-start.5
  75.1 3.6 %all_to_all.18 = f32[2,1,128]{2,1,0:T(1,128)S(1)} all-to-all(f32[2,1,128]{2,1,0:T(1,128)S(1)} %broadcast_in_dim.8), channel_id=1, replica_groups=mesh['node'=16,'board'=2] {'board'}, dimensions={0} | all-to-all | bytes 2048 | tf_op jit(solution)/shard_map/all_to_all | solution.py:361
  78.8 7.6 %all_to_all.19 = f32[4,1,128]{2,1,0:T(1,128)S(1)} all-to-all(f32[4,1,128]{2,1,0:T(1,128)S(1)} %broadcast_in_dim.9), channel_id=1, replica_groups={{0,2,4,6},{8,10,12,14},{16,18,20,22},{24,26,28,30},{1,3,5,7},{9,11,13,1..., dimensions={0} | all-to-all | bytes 4096 | tf_op jit(solution)/shard_map/all_to_all | solution.py:361
  86.4 10.0 %all_to_all.20 = f32[4,1,128]{2,1,0:T(1,128)S(1)} all-to-all(f32[4,1,128]{2,1,0:T(1,128)S(1)} %broadcast_in_dim.10), channel_id=1, replica_groups={{0,8,16,24},{2,10,18,26},{4,12,20,28},{6,14,22,30},{1,9,17,25},{3,11,19..., dimensions={0} | all-to-all | bytes 4096 | tf_op jit(solution)/shard_map/all_to_all | solution.py:361
  96.5 0.0 collective-permute-done.5.from_far_ref
  96.5 0.0 collective-permute-done.3.from_right_ref
  96.5 0.0 collective-permute-done.4.from_left_ref
  96.5 0.0 copy-done.1
  96.5 1.9 %last.1 = (f32[1,4,32,1326]{3,2,1,0:T(8,128)}, f32[1,4,32,1326]{3,2,1,0:T(8,128)}) custom-call(s32[4,32]{1,0:T(4,128)S(1)} %copy-done.5, f32[4,11,32,128]{3,2,1,0:T(8,128)S(1)} %get-tuple-element.21.own_ref, f32[11,32,128]{2,1,0:T(8,128)S(1)} %collective-permute-done.3.from_right_ref, f32[2,11,32,128]{3,2,1,0:T(8,128)S(1)} %collective-permute-done.4.from_left_ref, ...), custom_call_target="tpu_custom_call" | custom-call | tf_op jit(solution)/shard_map/last/pallas_call | solution.py:433
  (6 shorter events, 0.1 us)
Async XLA Ops:
  0.6 1.1 %copy-start = (f32[1,4,32,1326]{3,2,1,0:T(8,128)S(1)}, f32[1,4,32,1326]{3,2,1,0:T(8,128)}, u32[]{:S(2)}) copy-start(f32[1,4,32,1326]{3,2,1,0:T(8,128)} %logits_ref.3) | copy-start | bytes 2036740
  1.7 0.7 copy-start.8
  2.4 0.7 copy-start.9
  3.1 18.2 %copy-start.2 = (f32[1,1326]{1,0:T(1,128)S(1)}, f32[1,1326]{1,0:T(1,128)}, u32[]{:S(2)}) copy-start(f32[1,1326]{1,0:T(1,128)} %one_ref.3) | copy-start | bytes 15916
  3.1 18.2 %copy-start.3 = (f32[1,1326]{1,0:T(1,128)S(1)}, f32[1,1326]{1,0:T(1,128)}, u32[]{:S(2)}) copy-start(f32[1,1326]{1,0:T(1,128)} %two_ref.3) | copy-start | bytes 15916
  3.1 18.2 %copy-start.5 = (s32[4,32]{1,0:T(4,128)S(1)}, s32[4,32]{1,0:T(4,128)}, u32[]{:S(2)}) copy-start(s32[4,32]{1,0:T(4,128)} %parent_ref.3) | copy-start | bytes 1540
  3.3 18.0 %collective-permute-start.1 = (f32[2,11,32,128]{3,2,1,0:T(8,128)S(1)}, f32[2,11,32,128]{3,2,1,0:T(8,128)S(1)}, u32[]{:S(2)}, u32[]{:S(2)}) collective-permute-start(f32[2,11,32,128]{3,2,1,0:T(8,128)S(1)} %get-tuple-element.16), channel_id=1, source_target_pairs={{0,30},{2,0},{4,2},{6,4},{8,6},{10,8},{12,10},{14,12},{16,14},{18,... | collective-permute-start | bytes 1081352 | tf_op jit(solution)/shard_map/ppermute | solution.py:25
  10.3 11.0 %collective-permute-start = (f32[11,32,128]{2,1,0:T(8,128)S(1)}, f32[11,32,128]{2,1,0:T(8,128)S(1)}, u32[]{:S(2)}, u32[]{:S(2)}) collective-permute-start(f32[11,32,128]{2,1,0:T(8,128)S(1)} %get-tuple-element.15), channel_id=1, source_target_pairs={{0,2},{2,4},{4,6},{6,8},{8,10},{10,12},{12,14},{14,16},{16,18},{18... | collective-permute-start | bytes 540680 | tf_op jit(solution)/shard_map/ppermute | solution.py:25
  10.3 11.0 %collective-permute-start.2 = (f32[11,24,128]{2,1,0:T(8,128)S(1)}, f32[11,24,128]{2,1,0:T(8,128)S(1)}, u32[]{:S(2)}, u32[]{:S(2)}) collective-permute-start(f32[11,24,128]{2,1,0:T(8,128)S(1)} %get-tuple-element.17), channel_id=1, source_target_pairs={{0,28},{2,30},{4,0},{6,2},{8,4},{10,6},{12,8},{14,10},{16,12},{18,... | collective-permute-start | bytes 405512 | tf_op jit(solution)/shard_map/ppermute | solution.py:25
  11.4 0.7 copy-start.4
  12.1 0.7 copy-start.6
  12.8 0.7 copy-start.7
  21.4 75.1 %copy-start.1 = (f32[1,4,32,1326]{3,2,1,0:T(8,128)S(1)}, f32[1,4,32,1326]{3,2,1,0:T(8,128)}, u32[]{:S(2)}) copy-start(f32[1,4,32,1326]{3,2,1,0:T(8,128)} %logits_ref.3) | copy-start | bytes 2036740
  69.4 27.0 %collective-permute-start.4 = (f32[2,11,32,128]{3,2,1,0:T(8,128)S(1)}, f32[2,11,32,128]{3,2,1,0:T(8,128)S(1)}, u32[]{:S(2)}, u32[]{:S(2)}) collective-permute-start(f32[2,11,32,128]{3,2,1,0:T(8,128)S(1)} %get-tuple-element.23), channel_id=1, source_target_pairs={{0,2},{2,4},{4,6},{6,8},{8,10},{10,12},{12,14},{14,16},{16,18},{18... | collective-permute-start | bytes 1081352 | tf_op jit(solution)/shard_map/ppermute | solution.py:25
  69.5 26.9 %collective-permute-start.3 = (f32[11,32,128]{2,1,0:T(8,128)S(1)}, f32[11,32,128]{2,1,0:T(8,128)S(1)}, u32[]{:S(2)}, u32[]{:S(2)}) collective-permute-start(f32[11,32,128]{2,1,0:T(8,128)S(1)} %get-tuple-element.22), channel_id=1, source_target_pairs={{0,30},{2,0},{4,2},{6,4},{8,6},{10,8},{12,10},{14,12},{16,14},{18,... | collective-permute-start | bytes 540680 | tf_op jit(solution)/shard_map/ppermute | solution.py:25
  75.1 21.3 %collective-permute-start.5 = (f32[11,24,128]{2,1,0:T(8,128)S(1)}, f32[11,24,128]{2,1,0:T(8,128)S(1)}, u32[]{:S(2)}, u32[]{:S(2)}) collective-permute-start(f32[11,24,128]{2,1,0:T(8,128)S(1)} %get-tuple-element.24), channel_id=1, source_target_pairs={{0,4},{2,6},{4,8},{6,10},{8,12},{10,14},{12,16},{14,18},{16,20},{1... | collective-permute-start | bytes 405512 | tf_op jit(solution)/shard_map/ppermute | solution.py:25

commit v3 on v1

--- a/solution.py
+++ b/solution.py
@@ -356,9 +356,22 @@
 
 
 def shared_parts(part):
-    count = lax.axis_size("node") * lax.axis_size("board")
-    spread = jnp.broadcast_to(part, (count, LANES))
-    return lax.all_to_all(spread, ("node", "board"), 0, 0, tiled=True)
+    nodes = lax.axis_size("node")
+    boards = lax.axis_size("board")
+    near = part
+    for flip in range(2):
+        for turn in range(boards):
+            if flip == 0 and turn == 0:
+                continue
+            pairs = [
+                (node * boards + board, (node ^ flip) * boards + (board + turn) % boards)
+                for node in range(nodes)
+                for board in range(boards)
+            ]
+            near = near + lax.ppermute(part, ("node", "board"), pairs)
+    groups = [list(range(start, nodes, 2)) for start in range(2)]
+    spread = jnp.broadcast_to(near, (nodes // 2, LANES))
+    return lax.all_to_all(spread, "node", 0, 0, axis_index_groups=groups, tiled=True)
 
 
 def per_device(

time: 60.7 us -> 64.1 us (1.056)
  waiting for transfers between devices: 5.67 us -> 11.8 us
  blocking collectives: 25.1 us -> 21.3 us
  starting transfers between devices: 13.8 us -> 14.9 us
    ppermute x0 -> x6, waiting for transfers between devices: none -> 6.08 us  [shared_parts(): near = near + lax.ppermute(part, ('node', 'board'), pairs)]
    all_to_all x2, blocking collectives: 25.1 us -> 21.3 us  [shared_parts(): lax.all_to_all(spread, 'node', 0, 0, axis_index_groups=groups, tiled=True)]
    ppermute x0 -> x6, starting transfers between devices: none -> 3.79 us  [shared_parts(): near = near + lax.ppermute(part, ('node', 'board'), pairs)]
    ppermute x6, starting transfers between devices: 13.8 us -> 11.1 us  [passed_along(): return lax.ppermute(value, axis, pairs)]
  transfers between devices with their start and end apart: 6 -> 12, of which waited for: 1 -> 5; matrix products, arithmetic and copies ran while one was open for 0% -> 0% of each run, Pallas kernels for 4% -> 3%
where the time goes in v3:
time: 64.1 us; the launch traced here: 63.7 us
  blocking collectives  21.3 us (33%)
  starting transfers between devices  14.9 us (23%)
  waiting for transfers between devices  11.8 us (18%)
  Pallas kernels  10.4 us (16%)
  local copies, waits for them, and re-layouts  4.58 us (7%)
  between operations  0.74 us (1%)
    all_to_all x2, blocking collectives, shared_parts(): lax.all_to_all(spread, 'node', 0, 0, axis_index_groups=groups, tiled=True)  21.3 us
    ppermute x6, starting transfers between devices, passed_along(): return lax.ppermute(value, axis, pairs)  11.1 us
    ppermute x6, waiting for transfers between devices, shared_parts(): near = near + lax.ppermute(part, ('node', 'board'), pairs)  6.08 us
    ppermute x6, waiting for transfers between devices, passed_along(): return lax.ppermute(value, axis, pairs)  5.67 us
    unnamed x20, local copies, waits for them, and re-layouts  4.57 us
    ppermute x6, starting transfers between devices, shared_parts(): near = near + lax.ppermute(part, ('node', 'board'), pairs)  3.79 us
    pallas_call x1, Pallas kernels, per_device(): pl.pallas_call(functools.partial(first_kernel, node_count), out_shape=(ch...  3.37 us
    pallas_call x1, Pallas kernels, per_device(): pl.pallas_call(functools.partial(second_kernel, entry_count), out_shape=m...  2.83 us
  transfers between devices with their start and end apart: 12, of which 5 were waited for; matrix products, arithmetic and copies ran while one was open for 0% of the time, Pallas kernels for 3%

profile of v3, /device:TPU:0, one launch (start us, length us, event | category | flops | bytes accessed | tf_op | source)
XLA Modules:
  0.0 63.7 jit_solution(14729486957346985953)
XLA Ops:
  0.6 0.0 copy-start
  0.6 1.1 %copy-done = f32[1,4,32,1326]{3,2,1,0:T(8,128)S(1)} copy-done((f32[1,4,32,1326]{3,2,1,0:T(8,128)S(1)}, f32[1,4,32,1326]{3,2,1,0:T(8,128)}, u32[]{:S(2)}) %copy-start) | copy-done | bytes 678936
  1.7 0.0 copy-start.8
  1.7 0.7 %copy-done.8 = f32[4,32]{1,0:T(4,128)S(1)} copy-done((f32[4,32]{1,0:T(4,128)S(1)}, f32[4,32]{1,0:T(4,128)}, u32[]{:S(2)}) %copy-start.8) | copy-done | bytes 536
  2.4 0.0 copy-start.9
  2.4 0.7 %copy-done.9 = s32[4,32]{1,0:T(4,128)S(1)} copy-done((s32[4,32]{1,0:T(4,128)S(1)}, s32[4,32]{1,0:T(4,128)}, u32[]{:S(2)}) %copy-start.9) | copy-done | bytes 536
  3.1 0.0 copy-start.2
  3.1 0.0 copy-start.3
  3.1 0.0 copy-start.5
  3.1 0.2 pack.1
  3.3 7.0 %collective-permute-start.1 = (f32[2,11,32,128]{3,2,1,0:T(8,128)S(1)}, f32[2,11,32,128]{3,2,1,0:T(8,128)S(1)}, u32[]{:S(2)}, u32[]{:S(2)}) collective-permute-start(f32[2,11,32,128]{3,2,1,0:T(8,128)S(1)} %get-tuple-element.16), channel_id=1, source_target_pairs={{0,30},{2,0},{4,2},{6,4},{8,6},{10,8},{12,10},{14,12},{16,14},{18,... | collective-permute-start | bytes 1081352 | tf_op jit(solution)/shard_map/ppermute | solution.py:25
  10.3 0.0 collective-permute-start
  10.3 1.1 %collective-permute-start.2 = (f32[11,24,128]{2,1,0:T(8,128)S(1)}, f32[11,24,128]{2,1,0:T(8,128)S(1)}, u32[]{:S(2)}, u32[]{:S(2)}) collective-permute-start(f32[11,24,128]{2,1,0:T(8,128)S(1)} %get-tuple-element.17), channel_id=1, source_target_pairs={{0,28},{2,30},{4,0},{6,2},{8,4},{10,6},{12,8},{14,10},{16,12},{18,... | collective-permute-start | bytes 405512 | tf_op jit(solution)/shard_map/ppermute | solution.py:25
  11.4 0.0 copy-start.4
  11.4 0.7 %copy-done.4 = s32[2,1408]{1,0:T(2,128)S(1)} copy-done((s32[2,1408]{1,0:T(2,128)S(1)}, s32[2,1408]{1,0:T(2,128)}, u32[]{:S(2)}) %copy-start.4) | copy-done | bytes 11288
  12.1 0.0 copy-start.6
  12.1 0.7 %copy-done.6 = s32[1,1326]{1,0:T(1,128)S(1)} copy-done((s32[1,1326]{1,0:T(1,128)S(1)}, s32[1,1326]{1,0:T(1,128)}, u32[]{:S(2)}) %copy-start.6) | copy-done | bytes 5328
  12.8 0.0 copy-start.7
  12.8 0.7 %copy-done.7 = s32[1,1326]{1,0:T(1,128)S(1)} copy-done((s32[1,1326]{1,0:T(1,128)S(1)}, s32[1,1326]{1,0:T(1,128)}, u32[]{:S(2)}) %copy-start.7) | copy-done | bytes 5328
  13.5 2.1 %payoff.1.block_ref = bf16[2816,1408]{1,0:T(8,128)(2,1)S(1)} custom-call(s32[2,1408]{1,0:T(2,128)S(1)} %copy-done.4, s32[1,1326]{1,0:T(1,128)S(1)} %copy-done.6, s32[1,1326]{1,0:T(1,128)S(1)} %copy-done.7), custom_call_target="tpu_custom_call" | custom-call | flops 507510784 | bytes 7929856 | tf_op jit(solution)/shard_map/payoff/pallas_call | solution.py:63
  15.7 5.7 %collective-permute-done.2.from_far_ref = f32[11,24,128]{2,1,0:T(8,128)S(1)} collective-permute-done((f32[11,24,128]{2,1,0:T(8,128)S(1)}, f32[11,24,128]{2,1,0:T(8,128)S(1)}, u32[]{:S(2)}, u32[]{:S(2)}) %collective-permute-start.2) | collective-permute-done | bytes 135200 | tf_op jit(solution)/shard_map/ppermute | solution.py:25
  21.3 0.0 collective-permute-done.from_left_ref
  21.3 0.0 collective-permute-done.1.from_right_ref
  21.3 0.0 copy-done.2
  21.3 0.0 copy-done.3
  21.4 0.0 copy-done.5
  21.4 0.0 copy-start.1
  21.4 3.4 %first.1 = (f32[4,4,8,1408]{3,2,1,0:T(8,128)S(1)}, f32[4,4,8,1408]{3,2,1,0:T(8,128)S(1)}, f32[1,128]{1,0:T(1,128)S(1)}) custom-call(s32[4,32]{1,0:T(4,128)S(1)} %copy-done.5, f32[4,11,32,128]{3,2,1,0:T(8,128)S(1)} %get-tuple-element.14.home_ref, f32[11,32,128]{2,1,0:T(8,128)S(1)} %collective-permute-done.from_left_ref, ...), custom_call_target="tpu_custom_call" | custom-call | flops 1776287744 | bytes 11894784 | tf_op jit(solution)/shard_map/first/pallas_call | solution.py:405
  24.8 0.5 collective-permute-start.5
  25.3 0.5 collective-permute-start.4
  25.8 0.9 %collective-permute-start.3 = (f32[1,128]{1,0:T(1,128)S(1)}, f32[1,128]{1,0:T(1,128)S(1)}, u32[]{:S(2)}, u32[]{:S(2)}) collective-permute-start(f32[1,128]{1,0:T(1,128)S(1)} %get-tuple-element.20), channel_id=1, source_target_pairs={{0,1},{1,0},{2,3},{3,2},{4,5},{5,4},{6,7},{7,6},{8,9},{9,8},{10,11... | collective-permute-start | bytes 1544 | tf_op jit(solution)/shard_map/ppermute | solution.py:371
  26.7 1.1 %collective-permute-done.5 = f32[1,128]{1,0:T(1,128)S(1)} collective-permute-done((f32[1,128]{1,0:T(1,128)S(1)}, f32[1,128]{1,0:T(1,128)S(1)}, u32[]{:S(2)}, u32[]{:S(2)}) %collective-permute-start.5) | collective-permute-done | bytes 544 | tf_op jit(solution)/shard_map/ppermute | solution.py:371
  27.8 1.1 %collective-permute-done.4 = f32[1,128]{1,0:T(1,128)S(1)} collective-permute-done((f32[1,128]{1,0:T(1,128)S(1)}, f32[1,128]{1,0:T(1,128)S(1)}, u32[]{:S(2)}, u32[]{:S(2)}) %collective-permute-start.4) | collective-permute-done | bytes 544 | tf_op jit(solution)/shard_map/ppermute | solution.py:371
  28.8 0.0 collective-permute-done.3
  28.9 12.4 %all_to_all.16 = f32[8,1,128]{2,1,0:T(1,128)S(1)} all-to-all(f32[8,1,128]{2,1,0:T(1,128)S(1)} %broadcast_in_dim.4), channel_id=1, replica_groups={{0,4,8,12,16,20,24,28},{2,6,10,14,18,22,26,30},{1,5,9,13,17,21,25,29},{..., dimensions={0} | all-to-all | bytes 8192 | tf_op jit(solution)/shard_map/all_to_all | solution.py:374
  41.3 2.8 %second.1 = (f32[4,11,32,128]{3,2,1,0:T(8,128)S(1)}, f32[11,32,128]{2,1,0:T(8,128)S(1)}, f32[2,11,32,128]{3,2,1,0:T(8,128)S(1)}, f32[11,24,128]{2,1,0:T(8,128)S(1)}, f32[1,128]{1,0:T(1,128)S(1)}) custom-call(f32[4,4,8,1408]{3,2,1,0:T(8,128)S(1)} %get-tuple-element.18.chain_ref, f32[4,4,8,1408]{3,2,1,0:T(8,128)S(1)} %get-tuple-element.19.value_ref, ...), custom_call_target="tpu_custom_call" | custom-call | flops 1776287744 | bytes 11894784 | tf_op jit(solution)/shard_map/second/pallas_call | solution.py:415
  44.1 1.0 %collective-permute-start.7 = (f32[2,11,32,128]{3,2,1,0:T(8,128)S(1)}, f32[2,11,32,128]{3,2,1,0:T(8,128)S(1)}, u32[]{:S(2)}, u32[]{:S(2)}) collective-permute-start(f32[2,11,32,128]{3,2,1,0:T(8,128)S(1)} %get-tuple-element.23), channel_id=1, source_target_pairs={{0,2},{2,4},{4,6},{6,8},{8,10},{10,12},{12,14},{14,16},{16,18},{18... | collective-permute-start | bytes 1081352 | tf_op jit(solution)/shard_map/ppermute | solution.py:25
  45.2 0.0 collective-permute-start.11
  45.2 1.1 %collective-permute-start.10 = (f32[1,128]{1,0:T(1,128)S(1)}, f32[1,128]{1,0:T(1,128)S(1)}, u32[]{:S(2)}, u32[]{:S(2)}) collective-permute-start(f32[1,128]{1,0:T(1,128)S(1)} %get-tuple-element.25), channel_id=1, source_target_pairs={{0,2},{1,3},{2,0},{3,1},{4,6},{5,7},{6,4},{7,5},{8,10},{9,11},{10,... | collective-permute-start | bytes 1544 | tf_op jit(solution)/shard_map/ppermute | solution.py:371
  46.2 0.8 %collective-permute-start.9 = (f32[1,128]{1,0:T(1,128)S(1)}, f32[1,128]{1,0:T(1,128)S(1)}, u32[]{:S(2)}, u32[]{:S(2)}) collective-permute-start(f32[1,128]{1,0:T(1,128)S(1)} %get-tuple-element.25), channel_id=1, source_target_pairs={{0,1},{1,0},{2,3},{3,2},{4,5},{5,4},{6,7},{7,6},{8,9},{9,8},{10,11... | collective-permute-start | bytes 1544 | tf_op jit(solution)/shard_map/ppermute | solution.py:371
  47.0 0.7 %collective-permute-start.8 = (f32[11,24,128]{2,1,0:T(8,128)S(1)}, f32[11,24,128]{2,1,0:T(8,128)S(1)}, u32[]{:S(2)}, u32[]{:S(2)}) collective-permute-start(f32[11,24,128]{2,1,0:T(8,128)S(1)} %get-tuple-element.24), channel_id=1, source_target_pairs={{0,4},{2,6},{4,8},{6,10},{8,12},{10,14},{12,16},{14,18},{16,20},{1... | collective-permute-start | bytes 405512 | tf_op jit(solution)/shard_map/ppermute | solution.py:25
  47.8 3.8 %collective-permute-done.11 = f32[1,128]{1,0:T(1,128)S(1)} collective-permute-done((f32[1,128]{1,0:T(1,128)S(1)}, f32[1,128]{1,0:T(1,128)S(1)}, u32[]{:S(2)}, u32[]{:S(2)}) %collective-permute-start.11) | collective-permute-done | bytes 544 | tf_op jit(solution)/shard_map/ppermute | solution.py:371
  51.6 1.3 %collective-permute-start.6 = (f32[11,32,128]{2,1,0:T(8,128)S(1)}, f32[11,32,128]{2,1,0:T(8,128)S(1)}, u32[]{:S(2)}, u32[]{:S(2)}) collective-permute-start(f32[11,32,128]{2,1,0:T(8,128)S(1)} %get-tuple-element.22), channel_id=1, source_target_pairs={{0,30},{2,0},{4,2},{6,4},{8,6},{10,8},{12,10},{14,12},{16,14},{18,... | collective-permute-start | bytes 540680 | tf_op jit(solution)/shard_map/ppermute | solution.py:25
  52.8 0.1 collective-permute-done.10
  53.0 0.0 collective-permute-done.9
  53.0 8.8 %all_to_all.17 = f32[8,1,128]{2,1,0:T(1,128)S(1)} all-to-all(f32[8,1,128]{2,1,0:T(1,128)S(1)} %broadcast_in_dim.5), channel_id=1, replica_groups={{0,4,8,12,16,20,24,28},{2,6,10,14,18,22,26,30},{1,5,9,13,17,21,25,29},{..., dimensions={0} | all-to-all | bytes 8192 | tf_op jit(solution)/shard_map/all_to_all | solution.py:374
  61.8 0.0 collective-permute-done.8.from_far_ref
  61.8 0.0 collective-permute-done.6.from_right_ref
  61.8 0.0 collective-permute-done.7.from_left_ref
  61.8 0.0 copy-done.1
  61.8 1.9 %last.1 = (f32[1,4,32,1326]{3,2,1,0:T(8,128)}, f32[1,4,32,1326]{3,2,1,0:T(8,128)}) custom-call(s32[4,32]{1,0:T(4,128)S(1)} %copy-done.5, f32[4,11,32,128]{3,2,1,0:T(8,128)S(1)} %get-tuple-element.21.own_ref, f32[11,32,128]{2,1,0:T(8,128)S(1)} %collective-permute-done.6.from_right_ref, f32[2,11,32,128]{3,2,1,0:T(8,128)S(1)} %collective-permute-done.7.from_left_ref, ...), custom_call_target="tpu_custom_call" | custom-call | tf_op jit(solution)/shard_map/last/pallas_call | solution.py:429
  (4 shorter events, 0.0 us)
Async XLA Ops:
  0.6 1.1 %copy-start = (f32[1,4,32,1326]{3,2,1,0:T(8,128)S(1)}, f32[1,4,32,1326]{3,2,1,0:T(8,128)}, u32[]{:S(2)}) copy-start(f32[1,4,32,1326]{3,2,1,0:T(8,128)} %logits_ref.3) | copy-start | bytes 2036740
  1.7 0.7 %copy-start.8 = (f32[4,32]{1,0:T(4,128)S(1)}, f32[4,32]{1,0:T(4,128)}, u32[]{:S(2)}) copy-start(f32[4,32]{1,0:T(4,128)} %pot_ref.1) | copy-start | bytes 1540
  2.4 0.7 %copy-start.9 = (s32[4,32]{1,0:T(4,128)S(1)}, s32[4,32]{1,0:T(4,128)}, u32[]{:S(2)}) copy-start(s32[4,32]{1,0:T(4,128)} %kind_ref.1) | copy-start | bytes 1540
  3.1 18.2 %copy-start.2 = (f32[1,1326]{1,0:T(1,128)S(1)}, f32[1,1326]{1,0:T(1,128)}, u32[]{:S(2)}) copy-start(f32[1,1326]{1,0:T(1,128)} %one_ref.3) | copy-start | bytes 15916
  3.1 18.2 %copy-start.3 = (f32[1,1326]{1,0:T(1,128)S(1)}, f32[1,1326]{1,0:T(1,128)}, u32[]{:S(2)}) copy-start(f32[1,1326]{1,0:T(1,128)} %two_ref.3) | copy-start | bytes 15916
  3.1 18.2 %copy-start.5 = (s32[4,32]{1,0:T(4,128)S(1)}, s32[4,32]{1,0:T(4,128)}, u32[]{:S(2)}) copy-start(s32[4,32]{1,0:T(4,128)} %parent_ref.3) | copy-start | bytes 1540
  3.3 18.0 %collective-permute-start.1 = (f32[2,11,32,128]{3,2,1,0:T(8,128)S(1)}, f32[2,11,32,128]{3,2,1,0:T(8,128)S(1)}, u32[]{:S(2)}, u32[]{:S(2)}) collective-permute-start(f32[2,11,32,128]{3,2,1,0:T(8,128)S(1)} %get-tuple-element.16), channel_id=1, source_target_pairs={{0,30},{2,0},{4,2},{6,4},{8,6},{10,8},{12,10},{14,12},{16,14},{18,... | collective-permute-start | bytes 1081352 | tf_op jit(solution)/shard_map/ppermute | solution.py:25
  10.3 11.0 %collective-permute-start = (f32[11,32,128]{2,1,0:T(8,128)S(1)}, f32[11,32,128]{2,1,0:T(8,128)S(1)}, u32[]{:S(2)}, u32[]{:S(2)}) collective-permute-start(f32[11,32,128]{2,1,0:T(8,128)S(1)} %get-tuple-element.15), channel_id=1, source_target_pairs={{0,2},{2,4},{4,6},{6,8},{8,10},{10,12},{12,14},{14,16},{16,18},{18... | collective-permute-start | bytes 540680 | tf_op jit(solution)/shard_map/ppermute | solution.py:25
  10.3 11.0 %collective-permute-start.2 = (f32[11,24,128]{2,1,0:T(8,128)S(1)}, f32[11,24,128]{2,1,0:T(8,128)S(1)}, u32[]{:S(2)}, u32[]{:S(2)}) collective-permute-start(f32[11,24,128]{2,1,0:T(8,128)S(1)} %get-tuple-element.17), channel_id=1, source_target_pairs={{0,28},{2,30},{4,0},{6,2},{8,4},{10,6},{12,8},{14,10},{16,12},{18,... | collective-permute-start | bytes 405512 | tf_op jit(solution)/shard_map/ppermute | solution.py:25
  11.4 0.7 %copy-start.4 = (s32[2,1408]{1,0:T(2,128)S(1)}, s32[2,1408]{1,0:T(2,128)}, u32[]{:S(2)}) copy-start(s32[2,1408]{1,0:T(2,128)} %constant.2.clone.cards_ref) | copy-start | bytes 33796
  12.1 0.7 %copy-start.6 = (s32[1,1326]{1,0:T(1,128)S(1)}, s32[1,1326]{1,0:T(1,128)}, u32[]{:S(2)}) copy-start(s32[1,1326]{1,0:T(1,128)} %rank_ref.1) | copy-start | bytes 15916
  12.8 0.7 %copy-start.7 = (s32[1,1326]{1,0:T(1,128)S(1)}, s32[1,1326]{1,0:T(1,128)}, u32[]{:S(2)}) copy-start(s32[1,1326]{1,0:T(1,128)} %live_ref.1) | copy-start | bytes 15916
  21.4 40.5 %copy-start.1 = (f32[1,4,32,1326]{3,2,1,0:T(8,128)S(1)}, f32[1,4,32,1326]{3,2,1,0:T(8,128)}, u32[]{:S(2)}) copy-start(f32[1,4,32,1326]{3,2,1,0:T(8,128)} %logits_ref.3) | copy-start | bytes 2036740
  24.8 3.0 %collective-permute-start.5 = (f32[1,128]{1,0:T(1,128)S(1)}, f32[1,128]{1,0:T(1,128)S(1)}, u32[]{:S(2)}, u32[]{:S(2)}) collective-permute-start(f32[1,128]{1,0:T(1,128)S(1)} %get-tuple-element.20), channel_id=1, source_target_pairs={{0,3},{1,2},{2,1},{3,0},{4,7},{5,6},{6,5},{7,4},{8,11},{9,10},{10,... | collective-permute-start | bytes 1544 | tf_op jit(solution)/shard_map/ppermute | solution.py:371
  25.3 3.5 %collective-permute-start.4 = (f32[1,128]{1,0:T(1,128)S(1)}, f32[1,128]{1,0:T(1,128)S(1)}, u32[]{:S(2)}, u32[]{:S(2)}) collective-permute-start(f32[1,128]{1,0:T(1,128)S(1)} %get-tuple-element.20), channel_id=1, source_target_pairs={{0,2},{1,3},{2,0},{3,1},{4,6},{5,7},{6,4},{7,5},{8,10},{9,11},{10,... | collective-permute-start | bytes 1544 | tf_op jit(solution)/shard_map/ppermute | solution.py:371
  25.8 3.1 %collective-permute-start.3 = (f32[1,128]{1,0:T(1,128)S(1)}, f32[1,128]{1,0:T(1,128)S(1)}, u32[]{:S(2)}, u32[]{:S(2)}) collective-permute-start(f32[1,128]{1,0:T(1,128)S(1)} %get-tuple-element.20), channel_id=1, source_target_pairs={{0,1},{1,0},{2,3},{3,2},{4,5},{5,4},{6,7},{7,6},{8,9},{9,8},{10,11... | collective-permute-start | bytes 1544 | tf_op jit(solution)/shard_map/ppermute | solution.py:371
  44.1 17.7 %collective-permute-start.7 = (f32[2,11,32,128]{3,2,1,0:T(8,128)S(1)}, f32[2,11,32,128]{3,2,1,0:T(8,128)S(1)}, u32[]{:S(2)}, u32[]{:S(2)}) collective-permute-start(f32[2,11,32,128]{3,2,1,0:T(8,128)S(1)} %get-tuple-element.23), channel_id=1, source_target_pairs={{0,2},{2,4},{4,6},{6,8},{8,10},{10,12},{12,14},{14,16},{16,18},{18... | collective-permute-start | bytes 1081352 | tf_op jit(solution)/shard_map/ppermute | solution.py:25
  45.2 6.4 %collective-permute-start.11 = (f32[1,128]{1,0:T(1,128)S(1)}, f32[1,128]{1,0:T(1,128)S(1)}, u32[]{:S(2)}, u32[]{:S(2)}) collective-permute-start(f32[1,128]{1,0:T(1,128)S(1)} %get-tuple-element.25), channel_id=1, source_target_pairs={{0,3},{1,2},{2,1},{3,0},{4,7},{5,6},{6,5},{7,4},{8,11},{9,10},{10,... | collective-permute-start | bytes 1544 | tf_op jit(solution)/shard_map/ppermute | solution.py:371
  45.2 7.8 %collective-permute-start.10 = (f32[1,128]{1,0:T(1,128)S(1)}, f32[1,128]{1,0:T(1,128)S(1)}, u32[]{:S(2)}, u32[]{:S(2)}) collective-permute-start(f32[1,128]{1,0:T(1,128)S(1)} %get-tuple-element.25), channel_id=1, source_target_pairs={{0,2},{1,3},{2,0},{3,1},{4,6},{5,7},{6,4},{7,5},{8,10},{9,11},{10,... | collective-permute-start | bytes 1544 | tf_op jit(solution)/shard_map/ppermute | solution.py:371
  46.2 6.7 %collective-permute-start.9 = (f32[1,128]{1,0:T(1,128)S(1)}, f32[1,128]{1,0:T(1,128)S(1)}, u32[]{:S(2)}, u32[]{:S(2)}) collective-permute-start(f32[1,128]{1,0:T(1,128)S(1)} %get-tuple-element.25), channel_id=1, source_target_pairs={{0,1},{1,0},{2,3},{3,2},{4,5},{5,4},{6,7},{7,6},{8,9},{9,8},{10,11... | collective-permute-start | bytes 1544 | tf_op jit(solution)/shard_map/ppermute | solution.py:371
  47.0 14.8 %collective-permute-start.8 = (f32[11,24,128]{2,1,0:T(8,128)S(1)}, f32[11,24,128]{2,1,0:T(8,128)S(1)}, u32[]{:S(2)}, u32[]{:S(2)}) collective-permute-start(f32[11,24,128]{2,1,0:T(8,128)S(1)} %get-tuple-element.24), channel_id=1, source_target_pairs={{0,4},{2,6},{4,8},{6,10},{8,12},{10,14},{12,16},{14,18},{16,20},{1... | collective-permute-start | bytes 405512 | tf_op jit(solution)/shard_map/ppermute | solution.py:25
  51.6 10.3 %collective-permute-start.6 = (f32[11,32,128]{2,1,0:T(8,128)S(1)}, f32[11,32,128]{2,1,0:T(8,128)S(1)}, u32[]{:S(2)}, u32[]{:S(2)}) collective-permute-start(f32[11,32,128]{2,1,0:T(8,128)S(1)} %get-tuple-element.22), channel_id=1, source_target_pairs={{0,30},{2,0},{4,2},{6,4},{8,6},{10,8},{12,10},{14,12},{16,14},{18,... | collective-permute-start | bytes 540680 | tf_op jit(solution)/shard_map/ppermute | solution.py:25
